TPU v7x, 128 devices: a whole 4x4x4 slice. The times are simulated.
128 devices in a mesh: grp: 4 (over y), cur: 32 (over x, z, core).
Axes of the slice: x: 4, y: 4, z: 4, core: 2. Of those that a mesh axis runs over, the one named last changes fastest.
Arguments:
- fine_state: bfloat16 [786432, 256], P(('grp', 'cur')), may hold values from -8 to 8
- send_index: int32 [128, 2, 256], P(('grp', 'cur')), may hold values from 0 to 6143
- edge_src: int32 [128, 36864], P(('grp', 'cur')), may hold values from 0 to 6655, as said below
- edge_dst: int32 [128, 36864], P(('grp', 'cur')), may hold values from 0 to 6144, as said below
- cell_slot: int32 [786432], P(('grp', 'cur')), may hold values from 0 to 96, as said below
- slot_parent: int32 [128, 97], P(('grp', 'cur')), may hold values from 0 to 3071, as said below
- w_src: bfloat16 [256, 256], replicated, may hold values from -0.375 to 0.375
- w_dst: bfloat16 [256, 256], replicated, may hold values from -0.375 to 0.375
- msg_bias: float32 [256], replicated, may hold values from -4 to 4
- w_msg: bfloat16 [256, 256], replicated, may hold values from -0.375 to 0.375
- w_upd: bfloat16 [256, 256], replicated, may hold values from -0.375 to 0.375
- w_pool: bfloat16 [256, 1024], replicated, may hold values from -3 to 3
- norm_gain: float32 [1024], replicated, may hold values from 0.1 to 1.9
- w_query: bfloat16 [1024, 1024], replicated, may hold values from -1 to 1
- w_key: bfloat16 [1024, 256], replicated, may hold values from -1 to 1
- w_value: bfloat16 [1024, 256], replicated, may hold values from -0.1875 to 0.1875
- w_out: bfloat16 [1024, 1024], replicated, may hold values from -0.1875 to 0.1875
- head_scale: float32 [8], replicated, may hold values from 2 to 16
Outputs:
- fine_out: bfloat16 [786432, 256], P(('grp', 'cur'))
- coarse_out: bfloat16 [12288, 1024], P(('grp', 'cur'))
Inputs may be any that keep to these rules, and one draw needn't show every extreme that they name: `edge_src`: slots from a device's live count on hold 0; live slots name any entry of the device's table. `edge_dst`: the value 6144 marks a padded slot. On each device the live slots come first and number between half of 36864 and all of it; some device has all slots live. `cell_slot`: cells of one device that share a slot are consecutive and have one parent; every slot 0 to 96 is used on every device. `slot_parent`: A parent numbered p within its group is owned by the device of that group with cur index p // 96, at row p % 96. Each of a group's parents has exactly 64 cells, all on one device or on two consecutive devices of the group. On each device at most 4 slots name parents of one owner, and some owner receives exactly 4 from every device of its group.
All inputs are finite; a program needn't handle non-finite values.
Results may differ from a plain program's by a relative error of at most 0.005.
Values may be sent and summed in bfloat16 or wider, within the bound.
No kernel may reach another device: no remote copies, remote signals or barrier semaphores. Data moves between devices by JAX's collectives and lax.ppermute only.
A program may use at most 128 MiB of HBM per device.

v0:
```python
import math

import jax
import jax.numpy as jnp
from jax import lax
from jax.sharding import PartitionSpec as P

HEADS = 8
CHILD = 64


def passed_along(value, axis, by):
    devices = lax.axis_size(axis)
    return lax.ppermute(value, axis, [(i, (i + by) % devices) for i in range(devices)])


def body(
    fine_state,
    send_index,
    edge_src,
    edge_dst,
    cell_slot,
    slot_parent,
    w_src,
    w_dst,
    msg_bias,
    w_msg,
    w_upd,
    w_pool,
    norm_gain,
    w_query,
    w_key,
    w_value,
    w_out,
    head_scale,
):
    cell_count = fine_state.shape[0]
    width = fine_state.shape[1]
    rows_next = send_index[0, 0]
    rows_prev = send_index[0, 1]
    dst_proj = jnp.dot(fine_state, w_dst, preferred_element_type=jnp.float32).astype(jnp.bfloat16)
    before = passed_along(fine_state[rows_next], ("grp", "cur"), 1)
    after = passed_along(fine_state[rows_prev], ("grp", "cur"), -1)
    table = jnp.concatenate([fine_state, before, after], axis=0)
    src_proj = jnp.dot(table, w_src, preferred_element_type=jnp.float32).astype(jnp.bfloat16)
    edge_total = edge_src.shape[1]
    block = min(edge_total, 6144)
    source_blocks = edge_src.reshape(edge_total // block, block)
    target_blocks = edge_dst.reshape(edge_total // block, block)

    def edge_step(carry, inputs):
        source, target = inputs
        clipped = jnp.minimum(target, cell_count - 1)
        pre = (
            src_proj[source].astype(jnp.float32) + dst_proj[clipped].astype(jnp.float32) + msg_bias
        )
        hidden = jax.nn.silu(pre).astype(jnp.bfloat16)
        message = jnp.dot(hidden, w_msg, preferred_element_type=jnp.float32)
        return (carry + jax.ops.segment_sum(message, target, num_segments=cell_count + 1), None)

    start_sum = jnp.zeros((cell_count + 1, width), jnp.float32)
    summed, unused = lax.scan(edge_step, start_sum, (source_blocks, target_blocks))
    count = jax.ops.segment_sum(
        jnp.ones(edge_dst[0].shape, jnp.float32), edge_dst[0], num_segments=cell_count + 1
    )
    agg = (summed[:cell_count] / jnp.maximum(count[:cell_count], 1.0)[:, None]).astype(jnp.bfloat16)
    update = jnp.dot(agg, w_upd, preferred_element_type=jnp.float32)
    fine_out = (fine_state.astype(jnp.float32) + update).astype(jnp.bfloat16)
    slot_count = slot_parent.shape[1]
    par_dev = slot_count - 1
    onehot = (cell_slot[None, :] == jnp.arange(slot_count, dtype=jnp.int32)[:, None]).astype(
        jnp.bfloat16
    )
    partial_sum = jnp.dot(onehot, fine_out, preferred_element_type=jnp.float32)
    parents = slot_parent[0]
    owner = parents // par_dev
    local_row = parents % par_dev
    owners_count = lax.axis_size("cur")
    capacity = par_dev // owners_count + 1
    owner_hot = (owner[:, None] == jnp.arange(owners_count, dtype=jnp.int32)[None, :]).astype(
        jnp.int32
    )
    rank = jnp.sum((jnp.cumsum(owner_hot, axis=0) - owner_hot) * owner_hot, axis=1)
    outgoing = (
        jnp.zeros((owners_count, capacity, width), jnp.float32).at[owner, rank].set(partial_sum)
    )
    labels = jnp.full((owners_count, capacity), par_dev, jnp.int32).at[owner, rank].set(local_row)
    incoming, in_labels = (
        lax.all_to_all(outgoing, "cur", split_axis=0, concat_axis=0, tiled=True),
        lax.all_to_all(labels, "cur", split_axis=0, concat_axis=0, tiled=True),
    )
    flat = incoming.reshape(owners_count * capacity, width)
    pick = (jnp.arange(par_dev, dtype=jnp.int32)[:, None] == in_labels.reshape(1, -1)).astype(
        jnp.float32
    )
    parent_sum = jnp.dot(
        pick, flat, precision=lax.Precision.HIGHEST, preferred_element_type=jnp.float32
    )
    parent_mean = (parent_sum / float(CHILD)).astype(jnp.bfloat16)
    coarse = jnp.dot(parent_mean, w_pool, preferred_element_type=jnp.float32)
    inverse = lax.rsqrt(jnp.mean(coarse * coarse, axis=1, keepdims=True) + 1e-06)
    normed = (coarse * inverse * norm_gain).astype(jnp.bfloat16)
    query = jnp.dot(normed, w_query, preferred_element_type=jnp.float32).astype(jnp.bfloat16)
    keys = jnp.dot(normed, w_key, preferred_element_type=jnp.float32).astype(jnp.bfloat16)
    values = jnp.dot(normed, w_value, preferred_element_type=jnp.float32).astype(jnp.bfloat16)
    coarse_width = query.shape[1]
    head_size = coarse_width // HEADS
    kv_heads = keys.shape[1] // head_size
    per_group = HEADS // kv_heads
    queries4 = query.reshape(par_dev, kv_heads, per_group, head_size)
    factor = (head_scale * (1.0 / math.sqrt(head_size))).reshape(kv_heads, per_group)
    initial = (
        jnp.full((kv_heads, per_group, par_dev), -1e30, jnp.float32),
        jnp.zeros((kv_heads, per_group, par_dev), jnp.float32),
        jnp.zeros((kv_heads, per_group, par_dev, head_size), jnp.float32),
    )
    key_piece = lax.all_gather(keys, ("grp", "cur"), axis=0, tiled=True)
    value_piece = lax.all_gather(values, ("grp", "cur"), axis=0, tiled=True)
    total_rows = key_piece.shape[0]
    units = total_rows // par_dev
    step_units = max((u for u in range(1, units + 1) if units % u == 0 and u * par_dev <= 4096))
    block_rows = step_units * par_dev
    key_blocks = key_piece.reshape(total_rows // block_rows, block_rows, kv_heads, head_size)
    value_blocks = value_piece.reshape(total_rows // block_rows, block_rows, kv_heads, head_size)

    def inner(state, pair):
        running_top, running_norm, running_acc = state
        key_block, value_block = pair
        score = jnp.einsum(
            "qgrd,kgd->grqk", queries4, key_block, preferred_element_type=jnp.float32
        )
        score = score * factor[:, :, None, None]
        new_top = jnp.maximum(running_top, jnp.max(score, axis=-1))
        shrink = jnp.exp(running_top - new_top)
        weight = jnp.exp(score - new_top[..., None])
        new_norm = running_norm * shrink + jnp.sum(weight, axis=-1)
        product = jnp.einsum(
            "grqk,kgd->grqd",
            weight.astype(jnp.bfloat16),
            value_block,
            preferred_element_type=jnp.float32,
        )
        new_acc = running_acc * shrink[..., None] + product
        return ((new_top, new_norm, new_acc), None)

    result, unused_inner = lax.scan(inner, initial, (key_blocks, value_blocks))
    state = result
    final_top, final_norm, final_acc = state
    attn = final_acc / final_norm[..., None]
    attn = jnp.transpose(attn, (2, 0, 1, 3)).reshape(par_dev, coarse_width).astype(jnp.bfloat16)
    coarse_out = (coarse + jnp.dot(attn, w_out, preferred_element_type=jnp.float32)).astype(
        jnp.bfloat16
    )
    return (fine_out, coarse_out)


def solution(mesh):
    in_specs = (
        P(("grp", "cur"), None),
        P(("grp", "cur"), None, None),
        P(("grp", "cur"), None),
        P(("grp", "cur"), None),
        P(("grp", "cur")),
        P(("grp", "cur"), None),
        P(),
        P(),
        P(),
        P(),
        P(),
        P(),
        P(),
        P(),
        P(),
        P(),
        P(),
        P(),
    )
    out_specs = (P(("grp", "cur"), None), P(("grp", "cur"), None))
    return jax.shard_map(body, mesh=mesh, in_specs=in_specs, out_specs=out_specs, check_vma=False)
```

profile of v0, /device:TPU:0, one launch (start us, length us, event | category | flops | bytes accessed | tf_op | source)
XLA Modules:
  0.0 1168.9 jit_solution(14829304275574249346)
XLA Ops:
  14.7 8.3 collective-permute-start.1
  24.7 5.7 scatter_fusion.1
  44.7 210.0 %scatter_custom_fusion.1 = f32[6145]{0:T(1024)S(1)} fusion(s32[36864]{0:T(1024)} %bitcast.112, f32[36864]{0:T(1024)S(1)} %broadcast.252, f32[]{:T(128)} %constant.44.clone.1), kind=kCustom, calls=%fused_computation.66 | custom fusion | flops 36864 | bytes 25092 | tf_op jit(solution)/shard_map/scatter-add | solution.py:63
  263.0 605.3 %while.25 = (s32[]{:T(128)}, f32[6145,256]{1,0:T(8,128)}, s32[6,6144]{1,0:T(8,128)S(1)}, s32[6,6144]{1,0:T(8,128)S(1)}, bf16[6656,256]{1,0:T(8,128)(2,1)}, /*ind...) while((s32[]{:T(128)}, f32[6145,256]{1,0:T(8,128)}, ...), condition=%wide.region_2.3_spmd, body=%wide.region_0.2_spmd.sunk | while | flops 821090304 | bytes 44467296 | solution.py:62
  263.1 25.7 %gather_fusion = bf16[6144,256]{1,0:T(8,128)(2,1)} fusion(bf16[6144,256]{1,0:T(8,128)(2,1)} %get-tuple-element.327, s32[6144]{0:T(1024)S(1)} %broadcast_clamp_fusion.4), kind=kCustom, calls=%fused_computation.1.clone.1 | custom fusion | bytes 6316032 | tf_op jit(solution)/shard_map/while/body/eval_jaxpr/gather | solution.py:55
  288.8 25.8 %gather_fusion.1 = bf16[6144,256]{1,0:T(8,128)(2,1)} fusion(bf16[6656,256]{1,0:T(8,128)(2,1)} %get-tuple-element.326, s32[6144]{0:T(1024)S(1)} %broadcast_clamp_fusion.5), kind=kCustom, calls=%fused_computation.clone.1 | custom fusion | bytes 6316032 | tf_op jit(solution)/shard_map/while/body/eval_jaxpr/gather | solution.py:55
  314.6 7.6 fusion.60
  322.2 39.1 %scatter_fusion = f32[6145,256]{1,0:T(8,128)} fusion(f32[6145,256]{1,0:T(8,128)} %get-tuple-element.314, s32[6144]{0:T(1024)S(1)} %bitcast.109, f32[6144,256]{1,0:T(8,128)} %fusion.60), kind=kCustom, calls=%fused_computation.4.clone.1 | custom fusion | flops 1572864 | bytes 18898944 | tf_op jit(solution)/shard_map/while/body/eval_jaxpr/scatter-add | solution.py:59
  361.4 25.7 %gather_fusion = bf16[6144,256]{1,0:T(8,128)(2,1)} fusion(bf16[6144,256]{1,0:T(8,128)(2,1)} %get-tuple-element.327, s32[6144]{0:T(1024)S(1)} %broadcast_clamp_fusion.4), kind=kCustom, calls=%fused_computation.1.clone.1 | custom fusion | bytes 6316032 | tf_op jit(solution)/shard_map/while/body/eval_jaxpr/gather | solution.py:55
  387.0 25.8 %gather_fusion.1 = bf16[6144,256]{1,0:T(8,128)(2,1)} fusion(bf16[6656,256]{1,0:T(8,128)(2,1)} %get-tuple-element.326, s32[6144]{0:T(1024)S(1)} %broadcast_clamp_fusion.5), kind=kCustom, calls=%fused_computation.clone.1 | custom fusion | bytes 6316032 | tf_op jit(solution)/shard_map/while/body/eval_jaxpr/gather | solution.py:55
  412.8 7.6 fusion.60
  420.4 39.1 %scatter_fusion = f32[6145,256]{1,0:T(8,128)} fusion(f32[6145,256]{1,0:T(8,128)} %get-tuple-element.314, s32[6144]{0:T(1024)S(1)} %bitcast.109, f32[6144,256]{1,0:T(8,128)} %fusion.60), kind=kCustom, calls=%fused_computation.4.clone.1 | custom fusion | flops 1572864 | bytes 18898944 | tf_op jit(solution)/shard_map/while/body/eval_jaxpr/scatter-add | solution.py:59
  459.6 25.7 %gather_fusion = bf16[6144,256]{1,0:T(8,128)(2,1)} fusion(bf16[6144,256]{1,0:T(8,128)(2,1)} %get-tuple-element.327, s32[6144]{0:T(1024)S(1)} %broadcast_clamp_fusion.4), kind=kCustom, calls=%fused_computation.1.clone.1 | custom fusion | bytes 6316032 | tf_op jit(solution)/shard_map/while/body/eval_jaxpr/gather | solution.py:55
  485.3 25.8 %gather_fusion.1 = bf16[6144,256]{1,0:T(8,128)(2,1)} fusion(bf16[6656,256]{1,0:T(8,128)(2,1)} %get-tuple-element.326, s32[6144]{0:T(1024)S(1)} %broadcast_clamp_fusion.5), kind=kCustom, calls=%fused_computation.clone.1 | custom fusion | bytes 6316032 | tf_op jit(solution)/shard_map/while/body/eval_jaxpr/gather | solution.py:55
  511.1 7.6 fusion.60
  518.6 39.1 %scatter_fusion = f32[6145,256]{1,0:T(8,128)} fusion(f32[6145,256]{1,0:T(8,128)} %get-tuple-element.314, s32[6144]{0:T(1024)S(1)} %bitcast.109, f32[6144,256]{1,0:T(8,128)} %fusion.60), kind=kCustom, calls=%fused_computation.4.clone.1 | custom fusion | flops 1572864 | bytes 18898944 | tf_op jit(solution)/shard_map/while/body/eval_jaxpr/scatter-add | solution.py:59
  557.8 25.7 %gather_fusion = bf16[6144,256]{1,0:T(8,128)(2,1)} fusion(bf16[6144,256]{1,0:T(8,128)(2,1)} %get-tuple-element.327, s32[6144]{0:T(1024)S(1)} %broadcast_clamp_fusion.4), kind=kCustom, calls=%fused_computation.1.clone.1 | custom fusion | bytes 6316032 | tf_op jit(solution)/shard_map/while/body/eval_jaxpr/gather | solution.py:55
  583.5 25.8 %gather_fusion.1 = bf16[6144,256]{1,0:T(8,128)(2,1)} fusion(bf16[6656,256]{1,0:T(8,128)(2,1)} %get-tuple-element.326, s32[6144]{0:T(1024)S(1)} %broadcast_clamp_fusion.5), kind=kCustom, calls=%fused_computation.clone.1 | custom fusion | bytes 6316032 | tf_op jit(solution)/shard_map/while/body/eval_jaxpr/gather | solution.py:55
  609.3 7.6 fusion.60
  616.9 39.1 %scatter_fusion = f32[6145,256]{1,0:T(8,128)} fusion(f32[6145,256]{1,0:T(8,128)} %get-tuple-element.314, s32[6144]{0:T(1024)S(1)} %bitcast.109, f32[6144,256]{1,0:T(8,128)} %fusion.60), kind=kCustom, calls=%fused_computation.4.clone.1 | custom fusion | flops 1572864 | bytes 18898944 | tf_op jit(solution)/shard_map/while/body/eval_jaxpr/scatter-add | solution.py:59
  656.1 25.7 %gather_fusion = bf16[6144,256]{1,0:T(8,128)(2,1)} fusion(bf16[6144,256]{1,0:T(8,128)(2,1)} %get-tuple-element.327, s32[6144]{0:T(1024)S(1)} %broadcast_clamp_fusion.4), kind=kCustom, calls=%fused_computation.1.clone.1 | custom fusion | bytes 6316032 | tf_op jit(solution)/shard_map/while/body/eval_jaxpr/gather | solution.py:55
  681.8 25.8 %gather_fusion.1 = bf16[6144,256]{1,0:T(8,128)(2,1)} fusion(bf16[6656,256]{1,0:T(8,128)(2,1)} %get-tuple-element.326, s32[6144]{0:T(1024)S(1)} %broadcast_clamp_fusion.5), kind=kCustom, calls=%fused_computation.clone.1 | custom fusion | bytes 6316032 | tf_op jit(solution)/shard_map/while/body/eval_jaxpr/gather | solution.py:55
  707.6 7.6 fusion.60
  715.1 45.4 %scatter_fusion = f32[6145,256]{1,0:T(8,128)} fusion(f32[6145,256]{1,0:T(8,128)} %get-tuple-element.314, s32[6144]{0:T(1024)S(1)} %bitcast.109, f32[6144,256]{1,0:T(8,128)} %fusion.60), kind=kCustom, calls=%fused_computation.4.clone.1 | custom fusion | flops 1572864 | bytes 18898944 | tf_op jit(solution)/shard_map/while/body/eval_jaxpr/scatter-add | solution.py:59
  760.6 25.7 %gather_fusion = bf16[6144,256]{1,0:T(8,128)(2,1)} fusion(bf16[6144,256]{1,0:T(8,128)(2,1)} %get-tuple-element.327, s32[6144]{0:T(1024)S(1)} %broadcast_clamp_fusion.4), kind=kCustom, calls=%fused_computation.1.clone.1 | custom fusion | bytes 6316032 | tf_op jit(solution)/shard_map/while/body/eval_jaxpr/gather | solution.py:55
  786.3 25.8 %gather_fusion.1 = bf16[6144,256]{1,0:T(8,128)(2,1)} fusion(bf16[6656,256]{1,0:T(8,128)(2,1)} %get-tuple-element.326, s32[6144]{0:T(1024)S(1)} %broadcast_clamp_fusion.5), kind=kCustom, calls=%fused_computation.clone.1 | custom fusion | bytes 6316032 | tf_op jit(solution)/shard_map/while/body/eval_jaxpr/gather | solution.py:55
  812.1 7.6 fusion.60
  819.6 48.7 %scatter_fusion = f32[6145,256]{1,0:T(8,128)} fusion(f32[6145,256]{1,0:T(8,128)} %get-tuple-element.314, s32[6144]{0:T(1024)S(1)} %bitcast.109, f32[6144,256]{1,0:T(8,128)} %fusion.60), kind=kCustom, calls=%fused_computation.4.clone.1 | custom fusion | flops 1572864 | bytes 18898944 | tf_op jit(solution)/shard_map/while/body/eval_jaxpr/scatter-add | solution.py:59
  875.1 13.1 %scatter_fusion.2 = f32[32,4,256]{2,1,0:T(4,128)} fusion(f32[32,4,256]{2,1,0:T(4,128)} %broadcast_in_dim.23, s32[97]{0:T(128)S(1)} %copy-done.3, f32[97,256]{1,0:T(8,128)S(1)} %fusion.21), kind=kCustom, calls=%fused_computation.7 | custom fusion | bytes 298760 | tf_op jit(solution)/shard_map/scatter | solution.py:85
  888.2 32.2 %all-to-all-start.1 = ((f32[32,4,256]{2,1,0:T(4,128)}), f32[32,4,256]{2,1,0:T(4,128)S(1)}, u32[]{:S(2)}, u32[]{:S(2)}) async-start(f32[32,4,256]{2,1,0:T(4,128)} %scatter_fusion.2), calls=%async_computation.1 | async-start | bytes 262144 | tf_op jit(solution)/shard_map/all_to_all | solution.py:89
  922.0 6.3 all-to-all-done.1
  933.8 60.7 %all-gather.3.cloned.1.call-done = bf16[12288,256]{1,0:T(8,128)(2,1)} async-done(((bf16[96,256]{1,0:T(8,128)(2,1)}), bf16[12288,256]{1,0:T(8,128)(2,1)}) %all-gather.3.cloned.1.call-update) | async-done | bytes 6291472 | tf_op jit(solution)/shard_map/all_gather | solution.py:117
  994.5 9.7 reshape.241
  1004.2 59.1 %all-gather.5.cloned.1.call-done = bf16[12288,256]{1,0:T(8,128)(2,1)} async-done(((bf16[96,256]{1,0:T(8,128)(2,1)}), bf16[12288,256]{1,0:T(8,128)(2,1)}) %all-gather.5.cloned.1.call-update) | async-done | bytes 6291472 | tf_op jit(solution)/shard_map/all_gather | solution.py:118
  1063.3 9.7 reshape.243
  1073.1 85.8 %while.26 = (s32[]{:T(128)}, f32[2,4,96]{2,1,0:T(4,128)S(1)}, f32[2,4,96]{2,1,0:T(4,128)S(1)}, f32[2,4,96,128]{3,2,1,0:T(8,128)S(1)}, bf16[4,3072,2,128]{3,2,1,0...) while((s32[]{:T(128)}, f32[2,4,96]{2,1,0:T(4,128)S(1)}, ...), condition=%wide.region_12.13_spmd.clone, body=%wide.region_9.12_spmd.clone.sunk | while | flops 1227132672 | bytes 76529968 | solution.py:146
  1073.1 5.2 constant_dynamic-slice_fusion.5
  1078.4 6.4 bitcast_reduce_fusion.2
  1084.8 5.5 fusion.63
  1094.5 5.2 constant_dynamic-slice_fusion.5
  1099.8 6.4 bitcast_reduce_fusion.2
  1106.3 5.5 fusion.63
  1116.0 5.2 constant_dynamic-slice_fusion.5
  1121.3 6.4 bitcast_reduce_fusion.2
  1127.7 5.5 fusion.63
  1137.5 5.2 constant_dynamic-slice_fusion.5
  1142.8 6.4 bitcast_reduce_fusion.2
  1149.2 5.5 fusion.63
  (128 shorter events, 66.1 us)
Async XLA Ops:
  7.2 926.0 %copy-start = (bf16[1024,1024]{1,0:T(8,128)(2,1)S(1)}, bf16[1024,1024]{1,0:T(8,128)(2,1)}, u32[]{:S(2)}) copy-start(bf16[1024,1024]{1,0:T(8,128)(2,1)} %param.35) | copy-start | bytes 6291460
  7.2 32.9 %copy-start.5 = (bf16[256,256]{1,0:T(8,128)(2,1)S(1)}, bf16[256,256]{1,0:T(8,128)(2,1)}, u32[]{:S(2)}) copy-start(bf16[256,256]{1,0:T(8,128)(2,1)} %param.29) | copy-start | bytes 393220
  11.3 243.9 %collective-permute-start = (bf16[256,256]{1,0:T(8,128)(2,1)S(1)}, bf16[256,256]{1,0:T(8,128)(2,1)S(1)}, u32[]{:S(2)}, u32[]{:S(2)}) collective-permute-start(bf16[256,256]{1,0:T(8,128)(2,1)S(1)} %gather_fusion.2), channel_id=1, source_target_pairs={{0,1},{1,2},{2,3},{3,4},{4,5},{5,6},{6,7},{7,8},{8,9},{9,10},{10,1... | collective-permute-start | bytes 393224 | tf_op jit(solution)/shard_map/ppermute | solution.py:14
  14.7 240.6 %collective-permute-start.1 = (bf16[256,256]{1,0:T(8,128)(2,1)S(1)}, bf16[256,256]{1,0:T(8,128)(2,1)S(1)}, u32[]{:S(2)}, u32[]{:S(2)}) collective-permute-start(bf16[256,256]{1,0:T(8,128)(2,1)S(1)} %gather_fusion.3), channel_id=1, source_target_pairs={{0,127},{1,0},{2,1},{3,2},{4,3},{5,4},{6,5},{7,6},{8,7},{9,8},{10,... | collective-permute-start | bytes 393224 | tf_op jit(solution)/shard_map/ppermute | solution.py:14
  24.7 19.9 %copy-start.2 = (s32[97]{0:T(128)}, s32[97]{0:T(128)S(1)}, u32[]{:S(2)}) copy-start(s32[97]{0:T(128)S(1)} %fusion.32) | copy-start | bytes 1168
  31.2 857.0 %all-to-all-start = ((s32[32,1,4]{2,1,0:T(1,128)}), s32[32,1,4]{2,1,0:T(1,128)}, u32[]{:S(2)}, u32[]{:S(2)}) async-start(s32[32,1,4]{2,1,0:T(1,128)} %copy.29), calls=%async_computation | async-start | bytes 32768 | tf_op jit(solution)/shard_map/all_to_all | solution.py:90
  40.1 215.2 %copy-start.8 = (bf16[256,256]{1,0:T(8,128)(2,1)S(1)}, bf16[256,256]{1,0:T(8,128)(2,1)}, u32[]{:S(2)}) copy-start(bf16[256,256]{1,0:T(8,128)(2,1)} %param.28) | copy-start | bytes 393220
  259.9 3.1 copy-start.9
  259.9 3.1 copy-start.12
  263.0 605.3 %copy-start.6 = (f32[6144]{0:T(1024)S(1)}, f32[6144]{0:T(1024)}, u32[]{:S(2)}) copy-start(f32[6144]{0:T(1024)} %slice_maximum_fusion) | copy-start | bytes 73732
  263.0 605.3 %copy-start.10 = (bf16[256,256]{1,0:T(8,128)(2,1)S(1)}, bf16[256,256]{1,0:T(8,128)(2,1)}, u32[]{:S(2)}) copy-start(bf16[256,256]{1,0:T(8,128)(2,1)} %param.32) | copy-start | bytes 393220
  868.3 4.5 copy-start.11
  868.3 6.8 copy-start.3
  872.8 1.7 copy-start.14
  872.8 55.8 %copy-start.4 = (bf16[256,1024]{1,0:T(8,128)(2,1)S(1)}, bf16[256,1024]{1,0:T(8,128)(2,1)}, u32[]{:S(2)}) copy-start(bf16[256,1024]{1,0:T(8,128)(2,1)} %param.33) | copy-start | bytes 1572868
  872.8 56.1 %copy-start.7 = (f32[1024]{0:T(1024)S(1)}, f32[1024]{0:T(1024)}, u32[]{:S(2)}) copy-start(f32[1024]{0:T(1024)} %param.34) | copy-start | bytes 12292
  872.8 60.3 %copy-start.13 = (f32[8]{0:T(128)S(1)}, f32[8]{0:T(128)}, u32[]{:S(2)}) copy-start(f32[8]{0:T(128)} %param.39) | copy-start | bytes 100
  888.2 40.1 %all-to-all-start.1 = ((f32[32,4,256]{2,1,0:T(4,128)}), f32[32,4,256]{2,1,0:T(4,128)S(1)}, u32[]{:S(2)}, u32[]{:S(2)}) async-start(f32[32,4,256]{2,1,0:T(4,128)} %scatter_fusion.2), calls=%async_computation.1 | async-start | bytes 262144 | tf_op jit(solution)/shard_map/all_to_all | solution.py:89
  920.4 74.0 %all-gather.3.cloned.1.call-start = ((), (), s32[]{:S(2)}) async-start(), calls=%async_computation.2 | async-start | bytes 6340608 | tf_op jit(solution)/shard_map/all_gather | solution.py:117
  930.9 132.4 %all-gather.5.cloned.1.call-start = ((), (), s32[]{:S(2)}) async-start(), calls=%async_computation.3 | async-start | bytes 6340608 | tf_op jit(solution)/shard_map/all_gather | solution.py:118
  1084.8 6.4 copy-start.1
  1106.3 6.4 copy-start.1
  1127.7 6.4 copy-start.1
  1149.2 6.4 copy-start.1
Sparse Core Ops, SparseCore 0:
  931.1 63.3 all-gather.2
  997.5 65.8 all-gather.4
where the time goes:
time: 1170 us
  other arithmetic  492 us (42%)
  local copies, waits for them, and re-layouts  385 us (33%)
  waiting for transfers between devices  126 us (11%)
  matrix products  106 us (9%)
  starting transfers between devices  45.4 us (4%)
  between operations  14.4 us (1%)
    scatter-add x6, other arithmetic, edge_step(): jax.ops.segment_sum(message, target, num_segments=cell_count + 1)  250 us
    scatter-add x1, other arithmetic, body(): jax.ops.segment_sum(jnp.ones(edge_dst[0].shape, jnp.float32), edge_dst[0]...  210 us
    gather x6, local copies, waits for them, and re-layouts, edge_step(): src_proj[source].astype(jnp.float32) + dst_proj[clipped].astype(jnp.float32)  155 us
    gather x6, local copies, waits for them, and re-layouts, edge_step(): dst_proj[clipped].astype(jnp.float32)  154 us
    all_gather x1, waiting for transfers between devices, body(): key_piece = lax.all_gather(keys, ('grp', 'cur'), axis=0, tiled=True)  60.7 us
    all_gather x1, waiting for transfers between devices, body(): value_piece = lax.all_gather(values, ('grp', 'cur'), axis=0, tiled=True)  59.1 us
    dot_general x6, matrix products, edge_step(): message = jnp.dot(hidden, w_msg, preferred_element_type=jnp.float32)  45.4 us
    all_to_all x1, starting transfers between devices, body(): lax.all_to_all(outgoing, 'cur', split_axis=0, concat_axis=0, tiled=True)  32.2 us
  transfers between devices with their start and end apart: 6, of which 3 were waited for; matrix products, arithmetic and copies ran while one was open for 75% of the time, Pallas kernels for 0%

commit v1 on v0

v1 whole, which is shorter than its diff:
```python
import math
import jax, jax.numpy as jnp
from jax import lax
from jax.experimental import pallas as pl
from jax.experimental.pallas import tpu as pltpu
from jax.sharding import PartitionSpec as P

TILE = 256
BLOCK_SHIFT = 22
LOCAL_SHIFT = 13
SLOT_ROWS = 104
bf16, f32, i32 = jnp.bfloat16, jnp.float32, jnp.int32


def sort_edges(source, target, blocks):
    edges = source.shape[0]
    block = target >> 8
    last = (blocks - 1) << BLOCK_SHIFT | 511 << LOCAL_SHIFT
    key = jnp.where(target < blocks * TILE,
                    (block << BLOCK_SHIFT) | ((target & 255) << LOCAL_SHIFT) | source, last)
    block_ids = jnp.arange(blocks, dtype=i32)
    count = jnp.sum((block[None, :] == block_ids[:, None]).astype(i32), axis=1)
    spare = (-count) & (TILE - 1)
    lane = jnp.arange(TILE, dtype=i32)
    filler = jnp.where(lane[None, :] < spare[:, None], (block_ids[:, None] << BLOCK_SHIFT) | (256 << LOCAL_SHIFT), last)
    keys = jnp.sort(jnp.concatenate([key, filler.reshape(-1)]))
    tiles = jnp.sum((count + spare) // TILE)
    return keys, tiles


def fine_kernel(rows_ref, meta_ref, local_ref, slot_ref, tag_ref, own_ref, before_ref, after_ref, w_src_ref, w_dst_ref,
                bias_ref, w_msg_ref, w_upd_ref, out_ref, part_ref, table, dst, total, count, got_a, got_b):
    blocks = own_ref.shape[0] // TILE
    tiles_most = local_ref.shape[0]

    def put_table(place, rows):
        proj = jnp.dot(rows, w_src_ref[...], preferred_element_type=f32).astype(bf16).astype(f32) + bias_ref[...]
        table[pl.ds(2 * place, TILE, stride=2), :] = proj[:, :128]
        table[pl.ds(2 * place + 1, TILE, stride=2), :] = proj[:, 128:]

    def project(b, carry):
        at = pl.multiple_of(b * TILE, TILE)
        own = own_ref[pl.ds(at, TILE), :]
        put_table(at, own)
        dst[pl.ds(at, TILE), :] = jnp.dot(own, w_dst_ref[...], preferred_element_type=f32).astype(bf16)
        total[pl.ds(at, TILE), :] = jnp.zeros((TILE, 256), f32)
        count[b] = jnp.zeros((8, TILE), f32)
        return carry

    lax.fori_loop(0, blocks, project, 0)
    put_table(blocks * TILE, before_ref[...])
    put_table(blocks * TILE + TILE, after_ref[...])

    def fetch(tile, got):
        base = jnp.minimum(tile, tiles_most - 1) * TILE
        for i in range(TILE):
            got[2 * i:2 * i + 2, :] = table[pl.ds(rows_ref[base + i], 2), :]

    rows_iota = lax.broadcasted_iota(i32, (TILE, TILE), 0)

    def dense(tile, got):
        b = meta_ref[tile]
        at = pl.multiple_of(b * TILE, TILE)
        hot = (rows_iota == local_ref[tile]).astype(f32).astype(bf16)
        own = lax.dot_general(hot, dst[pl.ds(at, TILE), :], (((0,), (0,)), ((), ())), preferred_element_type=f32)
        pre = own + jnp.concatenate([got[pl.ds(0, TILE, stride=2), :], got[pl.ds(1, TILE, stride=2), :]], axis=1)
        half = 0.5 * pre
        hidden = (half + half * jnp.tanh(half)).astype(bf16)
        total[pl.ds(at, TILE), :] += jnp.dot(hot, hidden, preferred_element_type=f32)
        count[b] += lax.dot_general(jnp.ones((8, TILE), bf16), hot, (((1,), (1,)), ((), ())), preferred_element_type=f32)

    fetch(0, got_a)

    def step(j, carry):
        fetch(2 * j + 1, got_b)
        dense(2 * j, got_a)
        fetch(2 * j + 2, got_a)
        dense(2 * j + 1, got_b)
        return carry

    lax.fori_loop(0, meta_ref[tiles_most], step, 0)

    slots = lax.broadcasted_iota(i32, (SLOT_ROWS, TILE), 0)

    def finish(b, parts):
        at = pl.multiple_of(b * TILE, TILE)
        scale = 1.0 / jnp.maximum(count[b], 1.0)
        scale = jnp.transpose(jnp.concatenate([scale] * 16, axis=0))
        mean = total[pl.ds(at, TILE), :] * jnp.concatenate([scale, scale], axis=1)
        high = mean.astype(bf16)
        low = (mean - high.astype(f32)).astype(bf16)
        w_msg = w_msg_ref[...]
        agg = (jnp.dot(high, w_msg, preferred_element_type=f32) + jnp.dot(low, w_msg, preferred_element_type=f32)).astype(bf16)
        update = jnp.dot(agg, w_upd_ref[...], preferred_element_type=f32)
        new = (own_ref[pl.ds(at, TILE), :].astype(f32) + update).astype(bf16)
        out_ref[pl.ds(at, TILE), :] = new
        hot = (slots == slot_ref[b]).astype(f32).astype(bf16)
        return parts + jnp.dot(hot, new, preferred_element_type=f32)

    parts = lax.fori_loop(0, blocks, finish, tag_ref[...].astype(f32))
    part_ref[...] = parts.astype(bf16)


def fine_pass(own, before, after, source, target, cell_slot, tags, w_src, w_dst, bias, w_msg, w_upd):
    cells = own.shape[0]
    blocks = cells // TILE
    keys, tiles = sort_edges(source, target, blocks)
    tiles_most = keys.shape[0] // TILE
    rows = (keys & ((1 << LOCAL_SHIFT) - 1)) * 2
    local = ((keys >> LOCAL_SHIFT) & 511).reshape(tiles_most, 1, TILE)
    meta = jnp.concatenate([keys[::TILE] >> BLOCK_SHIFT, ((tiles + 1) // 2)[None]])
    smem = pl.BlockSpec(memory_space=pltpu.SMEM)
    vmem = pl.BlockSpec(memory_space=pltpu.VMEM)
    return pl.pallas_call(
        fine_kernel,
        out_shape=(jax.ShapeDtypeStruct(own.shape, bf16), jax.ShapeDtypeStruct((SLOT_ROWS, 256), bf16)),
        in_specs=[smem, smem] + [vmem] * 11,
        out_specs=(vmem, vmem),
        scratch_shapes=[
            pltpu.VMEM((2 * (cells + 2 * TILE), 128), f32),
            pltpu.VMEM((cells, 256), bf16),
            pltpu.VMEM((cells, 256), f32),
            pltpu.VMEM((blocks, 8, TILE), f32),
            pltpu.VMEM((2 * TILE, 128), f32),
            pltpu.VMEM((2 * TILE, 128), f32),
        ],
        compiler_params=pltpu.CompilerParams(vmem_limit_bytes=56 << 20),
        name="fine_cells",
    )(rows, meta, local, cell_slot.reshape(blocks, 1, TILE), tags, own, before, after, w_src, w_dst, bias.reshape(1, -1), w_msg, w_upd)


def moved(value, axis, pairs):
    return lax.ppermute(value, axis, pairs)


def ring_gather(value, move):
    return jnp.concatenate([value] + [move(value, by) for by in (1, 3, 2)], axis=0)


def gather_group(part):
    devices = lax.axis_size("cur")

    def along_z(value, by):
        return lax.ppermute(value, "cur", [(i, i // 8 * 8 + (i + 2 * by) % 8) for i in range(devices)])

    def along_x(value, by):
        return lax.ppermute(value, "cur", [(i, (i + 8 * by) % devices) for i in range(devices)])

    rows = ring_gather(part[None], along_z)
    rows = ring_gather(rows, along_x)
    return jnp.concatenate([rows, lax.ppermute(rows, "cur", [(i, i ^ 1) for i in range(devices)])], axis=0)


def normed_parents(first, label_ref, rows_ref, w_pool_ref, gain_ref, parents):
    ids = lax.broadcasted_iota(i32, (parents, rows_ref.shape[0]), 0) + first
    hot = (ids == label_ref[...]).astype(f32).astype(bf16)
    mean = (jnp.dot(hot, rows_ref[...], preferred_element_type=f32) * (1.0 / 64.0)).astype(bf16)
    coarse = jnp.dot(mean, w_pool_ref[...], preferred_element_type=f32)
    inverse = lax.rsqrt(jnp.mean(coarse * coarse, axis=1, keepdims=True) + 1e-06)
    return coarse, (coarse * inverse * gain_ref[...]).astype(bf16)


def query_kernel(first_ref, label_ref, rows_ref, w_pool_ref, gain_ref, w_query_ref, coarse_ref, query_ref):
    coarse, normed = normed_parents(first_ref[0], label_ref, rows_ref, w_pool_ref, gain_ref, query_ref.shape[0])
    coarse_ref[...] = coarse
    query_ref[...] = jnp.dot(normed, w_query_ref[...], preferred_element_type=f32).astype(bf16)


def key_kernel(label_ref, rows_ref, w_pool_ref, gain_ref, w_key_ref, w_value_ref, key_ref, value_ref):
    parents = value_ref.shape[1]
    coarse, normed = normed_parents(pl.program_id(0) * parents, label_ref, rows_ref, w_pool_ref, gain_ref, parents)
    keys = jnp.dot(normed, w_key_ref[...], preferred_element_type=f32)
    values = jnp.dot(normed, w_value_ref[...], preferred_element_type=f32).astype(bf16)
    ones = jnp.ones((parents, 128), bf16)
    for g in range(2):
        turned = jnp.transpose(keys[:, g * 128:(g + 1) * 128]).astype(bf16)
        key_ref[g] = jnp.concatenate([turned, turned], axis=0)
        value_ref[g] = jnp.concatenate([values[:, g * 128:(g + 1) * 128], ones], axis=1)


def attend_kernel(factor_ref, query_ref, key_ref, value_ref, out_ref):
    rows = query_ref.shape[0]
    stats = []
    for g in range(2):
        scaled = jnp.concatenate(
            [query_ref[:, h * 128:(h + 1) * 128].astype(f32) * factor_ref[h] for h in range(4 * g, 4 * g + 4)], axis=0
        )
        high = scaled.astype(bf16)
        low = (scaled - high.astype(f32)).astype(bf16)
        score = jnp.dot(jnp.concatenate([high, low], axis=1), key_ref[g], preferred_element_type=f32)
        top = jnp.max(score, axis=1, keepdims=True)
        weight = jnp.exp2(score - top).astype(bf16)
        both = jnp.dot(weight, value_ref[g], preferred_element_type=f32)
        norm = both[:, 128:]
        attn = (both[:, :128] / norm).astype(bf16)
        level = top + jnp.log2(norm)
        for r in range(4):
            h = 4 * g + r
            out_ref[:, h * 128:(h + 1) * 128] = attn[r * rows:(r + 1) * rows]
            stats.append(level[r * rows:(r + 1) * rows])
    lanes = lax.broadcasted_iota(i32, (rows, 128), 1)
    level = jnp.zeros((rows, 128), f32)
    for h in range(8):
        level = jnp.where(lanes == h, stats[h], level)
    high = level.astype(bf16)
    rest = level - high.astype(f32)
    middle = rest.astype(bf16)
    low = (rest - middle.astype(f32)).astype(bf16)
    out_ref[:, 1024:1152] = high
    out_ref[:, 1152:1280] = middle
    out_ref[:, 1280:1408] = low


def merge_kernel(a_ref, b_ref, c_ref, d_ref, coarse_ref, w_out_ref, out_ref):
    refs = (a_ref, b_ref, c_ref, d_ref)
    levels = [r[:, 1024:1152].astype(f32) + (r[:, 1152:1280].astype(f32) + r[:, 1280:1408].astype(f32)) for r in refs]
    top = jnp.maximum(jnp.maximum(levels[0], levels[1]), jnp.maximum(levels[2], levels[3]))
    shares = [jnp.exp2(level - top) for level in levels]
    whole = shares[0] + shares[1] + shares[2] + shares[3]
    shares = [share / whole for share in shares]
    pieces = []
    for h in range(8):
        at = slice(h * 128, (h + 1) * 128)
        pieces.append(sum(r[:, at].astype(f32) * s[:, h:h + 1] for r, s in zip(refs, shares)))
    attn = jnp.concatenate(pieces, axis=1).astype(bf16)
    out_ref[...] = (coarse_ref[...] + jnp.dot(attn, w_out_ref[...], preferred_element_type=f32)).astype(bf16)


def body(fine_state, send_index, edge_src, edge_dst, cell_slot, slot_parent, w_src, w_dst, msg_bias, w_msg, w_upd,
         w_pool, norm_gain, w_query, w_key, w_value, w_out, head_scale):
    groups, devices = lax.axis_size("grp"), lax.axis_size("cur")
    smem = pl.BlockSpec(memory_space=pltpu.SMEM)
    vmem = pl.BlockSpec(memory_space=pltpu.VMEM)
    every = groups * devices
    both = ("grp", "cur")
    before = lax.ppermute(fine_state[send_index[0, 0]], both, [(i, (i + 1) % every) for i in range(every)])
    after = lax.ppermute(fine_state[send_index[0, 1]], both, [(i, (i - 1) % every) for i in range(every)])
    slots = slot_parent.shape[1]
    par_dev = slots - 1
    parents = jnp.full((256,), -64, i32).at[:slots].set(slot_parent[0])
    tags = jnp.zeros((SLOT_ROWS, 256), i32).at[slots].set(parents >> 6).at[slots + 1].set(parents & 63).astype(bf16)
    fine_out, part = fine_pass(fine_state, before, after, edge_src[0], edge_dst[0], cell_slot, tags,
                               w_src, w_dst, msg_bias, w_msg, w_upd)
    blocks = gather_group(part)
    labels = (blocks[:, slots, :SLOT_ROWS].astype(i32) * 64 + blocks[:, slots + 1, :SLOT_ROWS].astype(i32)).reshape(1, -1)
    rows = blocks.reshape(-1, 256)
    gain = norm_gain.reshape(1, -1)
    width = w_query.shape[1]
    params = pltpu.CompilerParams(vmem_limit_bytes=56 << 20)
    coarse, query = pl.pallas_call(
        query_kernel,
        out_shape=(jax.ShapeDtypeStruct((par_dev, width), f32), jax.ShapeDtypeStruct((par_dev, width), bf16)),
        in_specs=[smem] + [vmem] * 5,
        out_specs=(vmem, vmem),
        compiler_params=params,
        name="own_query",
    )((lax.axis_index("cur") * par_dev)[None], labels, rows, w_pool, gain, w_query)
    asked = {by: lax.ppermute(query, "grp", [(i, (i + by) % groups) for i in range(groups)]) for by in (2, 1, 3)}
    asked[0] = query
    known = par_dev * devices
    step = 512
    whole = lambda *shape: pl.BlockSpec(shape, lambda i: (0,) * len(shape))
    keys, values = pl.pallas_call(
        key_kernel,
        out_shape=(jax.ShapeDtypeStruct((2, 256, known), bf16), jax.ShapeDtypeStruct((2, known, 256), bf16)),
        grid=(known // step,),
        in_specs=[whole(*labels.shape), whole(*rows.shape), whole(*w_pool.shape), whole(*gain.shape),
                  whole(*w_key.shape), whole(*w_value.shape)],
        out_specs=(pl.BlockSpec((2, 256, step), lambda i: (0, 0, i)), pl.BlockSpec((2, step, 256), lambda i: (0, i, 0))),
        compiler_params=params,
        name="group_keys",
    )(labels, rows, w_pool, gain, w_key, w_value)
    factor = head_scale * (math.log2(math.e) / math.sqrt(128.0))
    found = []
    for by in (2, 1, 3, 0):
        piece = pl.pallas_call(
            attend_kernel,
            out_shape=jax.ShapeDtypeStruct((par_dev, width + 384), bf16),
            in_specs=[smem] + [vmem] * 3,
            out_specs=vmem,
            compiler_params=params,
            name="attend",
        )(factor, asked[by], keys, values)
        if by:
            piece = lax.ppermute(piece, "grp", [(i, (i - by) % groups) for i in range(groups)])
        found.append(piece)
    coarse_out = pl.pallas_call(
        merge_kernel,
        out_shape=jax.ShapeDtypeStruct((par_dev, width), bf16),
        in_specs=[vmem] * 6,
        out_specs=vmem,
        compiler_params=params,
        name="merge",
    )(*found, coarse, w_out)
    return fine_out, coarse_out


def solution(mesh):
    line = P(("grp", "cur"), None)
    in_specs = (line, P(("grp", "cur"), None, None), line, line, P(("grp", "cur")), line) + (P(),) * 12
    return jax.shard_map(body, mesh=mesh, in_specs=in_specs, out_specs=(line, line), check_vma=False)
```

time: 1170 us -> 238 us (0.20)
  other arithmetic: 492 us -> 31.1 us
  local copies, waits for them, and re-layouts: 385 us -> 12.4 us
  Pallas kernels: 0 us -> 151 us
  waiting for transfers between devices: 126 us -> 15.1 us
  matrix products: 106 us -> 0 us
  starting transfers between devices: 45.4 us -> 23.7 us
  between operations: 14.4 us -> 1.78 us
    scatter-add x7 -> x0, other arithmetic: 460 us -> none  [the longest x6 250 us: edge_step(): jax.ops.segment_sum(message, target, num_segments=cell_count + 1)]
    gather x14 -> x2, local copies, waits for them, and re-layouts: 315 us -> 6.53 us  [the longest x1 3.26 us: body(): fine_state[send_index[0, 0]]]
    pallas_call x0 -> x8, Pallas kernels: none -> 151 us  [the longest x1 87.6 us: fine_pass(): pl.pallas_call(fine_kernel, out_shape=(jax.ShapeDtypeStruct(own.shape, bf...]
    all_gather x2 -> x0, waiting for transfers between devices: 120 us -> none  [the longest x1 60.7 us: body(): key_piece = lax.all_gather(keys, ('grp', 'cur'), axis=0, tiled=True)]
    dot_general x24 -> x0, matrix products: 106 us -> none  [the longest x6 45.4 us: edge_step(): message = jnp.dot(hidden, w_msg, preferred_element_type=jnp.float32)]
    all_to_all x2 -> x0, starting transfers between devices: 36.7 us -> none  [the longest x1 32.2 us: body(): lax.all_to_all(outgoing, 'cur', split_axis=0, concat_axis=0, tiled=True)]
    sort x0 -> x1, other arithmetic: none -> 25.2 us  [sort_edges(): keys = jnp.sort(jnp.concatenate([key, filler.reshape(-1)]))]
    reduce_sum x5 -> x2, other arithmetic: 22.2 us -> 1.1 us  [the longest x1 0.65 us: sort_edges(): tiles = jnp.sum((count + spare) // TILE)]
  transfers between devices with their start and end apart: 6 -> 15, of which waited for: 3 -> 7; matrix products, arithmetic and copies ran while one was open for 75% -> 14% of each run, Pallas kernels for 0% -> 23%
where the time goes in v1:
time: 238 us; the launch traced here: 235 us
  Pallas kernels  151 us (63%)
  other arithmetic  31.1 us (13%)
  starting transfers between devices  23.7 us (10%)
  waiting for transfers between devices  15.1 us (6%)
  local copies, waits for them, and re-layouts  12.4 us (5%)
    pallas_call x1, Pallas kernels, fine_pass(): pl.pallas_call(fine_kernel, out_shape=(jax.ShapeDtypeStruct(own.shape, bf...  87.6 us
    pallas_call x4, Pallas kernels, body(): pl.pallas_call(attend_kernel, out_shape=jax.ShapeDtypeStruct((par_dev, wi...  30.6 us
    sort x1, other arithmetic, sort_edges(): keys = jnp.sort(jnp.concatenate([key, filler.reshape(-1)]))  25.2 us
    pallas_call x1, Pallas kernels, body(): pl.pallas_call(key_kernel, out_shape=(jax.ShapeDtypeStruct((2, 256, known...  24.5 us
    ppermute x1, starting transfers between devices, body(): lax.ppermute(fine_state[send_index[0, 1]], both, [(i, (i - 1) % every) fo...  8.8 us
    ppermute x3, waiting for transfers between devices, along_x(): lax.ppermute(value, 'cur', [(i, (i + 8 * by) % devices) for i in range(de...  7.23 us
    ppermute x3, waiting for transfers between devices, along_z(): lax.ppermute(value, 'cur', [(i, i // 8 * 8 + (i + 2 * by) % 8) for i in r...  4.96 us
  transfers between devices with their start and end apart: 15, of which 7 were waited for; matrix products, arithmetic and copies ran while one was open for 14% of the time, Pallas kernels for 23%

profile of v1, /device:TPU:0, one launch (start us, length us, event | category | flops | bytes accessed | tf_op | source)
XLA Modules:
  0.0 234.9 jit_solution(6414104261506578040)
XLA Ops:
  0.7 0.8 compare_select_fusion.1
  1.4 3.3 %gather_fusion = bf16[256,256]{1,0:T(8,128)(2,1)S(1)} fusion(bf16[6144,256]{1,0:T(8,128)(2,1)} %own_ref.1, s32[1024]{0:T(1024)S(1)} %get-tuple-element.79), kind=kCustom, calls=%fused_computation | custom fusion | bytes 263168 | tf_op jit(solution)/shard_map/gather | solution.py:236
  4.8 3.3 %gather_fusion.1 = bf16[256,256]{1,0:T(8,128)(2,1)S(1)} fusion(bf16[6144,256]{1,0:T(8,128)(2,1)} %own_ref.1, s32[1024]{0:T(1024)S(1)} %get-tuple-element.78), kind=kCustom, calls=%fused_computation.1 | custom fusion | bytes 263168 | tf_op jit(solution)/shard_map/gather | solution.py:237
  8.0 8.8 %collective-permute-start.1 = (bf16[256,256]{1,0:T(8,128)(2,1)S(1)}, bf16[256,256]{1,0:T(8,128)(2,1)S(1)}, u32[]{:S(2)}, u32[]{:S(2)}) collective-permute-start(bf16[256,256]{1,0:T(8,128)(2,1)S(1)} %gather_fusion.1), channel_id=1, source_target_pairs={{0,127},{1,0},{2,1},{3,2},{4,3},{5,4},{6,5},{7,6},{8,7},{9,8},{10,... | collective-permute-start | bytes 393224 | tf_op jit(solution)/shard_map/ppermute | solution.py:237
  16.9 0.4 compare_select_fusion
  17.2 0.5 convert_reduce_fusion
  17.7 0.6 fusion.3
  18.5 25.2 %sort.15 = (s32[43008]{0:T(1024)S(1)}, s32[43008]{0:T(1024)}) sort(s32[43008]{0:T(1024)S(1)} %pad_add_fusion, s32[43008]{0:T(1024)S(1)} %iota.15), dimensions={0}, to_apply=%region_1.0 | sort | flops 688128 | bytes 688128 | tf_op jit(solution)/shard_map/jit(sort)/sort | solution.py:26
  43.7 0.2 slice.55
  43.9 0.8 shift-right-arithmetic_and_fusion
  45.4 0.6 convert_element_type.29.tag_ref
  46.0 0.7 pad_add_fusion.1.meta_ref
  46.7 0.6 copy-done.9
  47.4 87.6 %fine_cells.1 = (bf16[6144,256]{1,0:T(8,128)(2,1)}, bf16[104,256]{1,0:T(8,128)(2,1)}) custom-call(s32[43008]{0:T(1024)} %get-tuple-element.60.rows_ref, s32[169]{0:T(256)} %pad_add_fusion.1.meta_ref, s32[168,1,256]{2,1,0:T(1,128)} %bitcast.26, s32[24,1,256]{2,1,0:T(1,128)} %bitcast.34, bf16[104,256]{1,0:T(8,128)(2,1)} %convert_element_type.29.tag_ref, ...), custom_call_target="tpu_custom_call" | custom-call | tf_op jit(solution)/shard_map/fine_cells/pallas_call | solution.py:114
  135.0 0.7 collective-permute-start.2
  135.7 2.5 %collective-permute-start.3 = (bf16[1,104,256]{2,1,0:T(8,128)(2,1)}, bf16[1,104,256]{2,1,0:T(8,128)(2,1)S(1)}, u32[]{:S(2)}, u32[]{:S(2)}) collective-permute-start(bf16[1,104,256]{2,1,0:T(8,128)(2,1)} %bitcast.30), channel_id=1, source_target_pairs={{0,6},{1,7},{2,0},{3,1},{4,2},{5,3},{6,4},{7,5},{8,14},{9,15},{10,... | collective-permute-start | bytes 159752 | tf_op jit(solution)/shard_map/ppermute | solution.py:144
  138.2 0.9 constant_dynamic-update-slice_fusion.6
  139.1 1.4 collective-permute-done.2
  140.6 3.5 %collective-permute-done.4 = bf16[1,104,256]{2,1,0:T(8,128)(2,1)S(1)} collective-permute-done((bf16[1,104,256]{2,1,0:T(8,128)(2,1)}, bf16[1,104,256]{2,1,0:T(8,128)(2,1)S(1)}, u32[]{:S(2)}, u32[]{:S(2)}) %collective-permute-start.4) | collective-permute-done | bytes 53280 | tf_op jit(solution)/shard_map/ppermute | solution.py:144
  144.1 0.8 pad_maximum_fusion
  145.0 3.2 %collective-permute-start.6 = (bf16[4,104,256]{2,1,0:T(8,128)(2,1)S(1)}, bf16[4,104,256]{2,1,0:T(8,128)(2,1)S(1)}, u32[]{:S(2)}, u32[]{:S(2)}) collective-permute-start(bf16[4,104,256]{2,1,0:T(8,128)(2,1)S(1)} %pad_maximum_fusion), channel_id=1, source_target_pairs={{0,24},{1,25},{2,26},{3,27},{4,28},{5,29},{6,30},{7,31},{8,0},{9,1... | collective-permute-start | bytes 638984 | tf_op jit(solution)/shard_map/ppermute | solution.py:147
  148.3 3.8 %collective-permute-done.5 = bf16[4,104,256]{2,1,0:T(8,128)(2,1)S(1)} collective-permute-done((bf16[4,104,256]{2,1,0:T(8,128)(2,1)S(1)}, bf16[4,104,256]{2,1,0:T(8,128)(2,1)S(1)}, u32[]{:S(2)}, u32[]{:S(2)}) %collective-permute-start.5) | collective-permute-done | bytes 213024 | tf_op jit(solution)/shard_map/ppermute | solution.py:147
  152.1 1.8 collective-permute-done.6
  153.9 1.7 collective-permute-done.7
  155.7 2.4 %collective-permute-done.8 = bf16[16,104,256]{2,1,0:T(8,128)(2,1)S(1)} collective-permute-done((bf16[16,104,256]{2,1,0:T(8,128)(2,1)S(1)}, bf16[16,104,256]{2,1,0:T(8,128)(2,1)S(1)}, u32[]{:S(2)}, u32[]{:S(2)}) %collective-permute-start.8) | collective-permute-done | bytes 852000 | tf_op jit(solution)/shard_map/ppermute | solution.py:151
  158.1 0.1 fusion.1
  158.2 0.9 add.56.label_ref
  159.1 0.2 copy-done
  159.3 4.4 %own_query.1 = (f32[96,1024]{1,0:T(8,128)}, bf16[96,1024]{1,0:T(8,128)(2,1)}) custom-call(s32[1]{0:T(128)} %bitcast.13.first_ref, s32[1,3328]{1,0:T(1,128)} %add.56.label_ref, bf16[3328,256]{1,0:T(8,128)(2,1)} %bitcast.24, bf16[256,1024]{1,0:T(8,128)(2,1)} %w_pool_ref.3, f32[1,1024]{1,0:T(1,128)} %bitcast.35, bf16[1024,1024]{1,0:T(8,128)(2,1)} %w_query_ref.1), custom_call_target="tpu_custom_call" | custom-call | tf_op jit(solution)/shard_map/own_query/pallas_call | solution.py:250
  163.8 1.9 collective-permute-start.11
  165.8 2.0 collective-permute-start.9
  167.8 0.5 broadcast_multiply_fusion.factor_ref
  168.4 24.5 %group_keys.1 = (bf16[2,256,3072]{2,1,0:T(8,128)(2,1)}, bf16[2,3072,256]{2,1,0:T(8,128)(2,1)}) custom-call(s32[1,3328]{1,0:T(1,128)} %add.56.label_ref, bf16[3328,256]{1,0:T(8,128)(2,1)} %bitcast.25, bf16[256,1024]{1,0:T(8,128)(2,1)} %w_pool_ref.3, f32[1,1024]{1,0:T(1,128)} %bitcast.36, bf16[1024,256]{1,0:T(8,128)(2,1)} %w_key_ref.1, ...), custom_call_target="tpu_custom_call" | custom-call | tf_op jit(solution)/shard_map/group_keys/pallas_call | solution.py:263
  192.8 0.7 copy-done.6
  193.5 7.7 %attend.6 = bf16[96,1408]{1,0:T(8,128)(2,1)} custom-call(f32[8]{0:T(128)} %broadcast_multiply_fusion.factor_ref, bf16[96,1024]{1,0:T(8,128)(2,1)} %copy-done.6, bf16[2,256,3072]{2,1,0:T(8,128)(2,1)} %get-tuple-element.50.key_ref, bf16[2,3072,256]{2,1,0:T(8,128)(2,1)} %get-tuple-element.51.value_ref), custom_call_target="tpu_custom_call" | custom-call | tf_op jit(solution)/shard_map/attend/pallas_call | solution.py:276
  201.2 0.1 collective-permute-start.14
  201.3 0.7 copy-done.5
  202.0 7.7 %attend.5 = bf16[96,1408]{1,0:T(8,128)(2,1)} custom-call(f32[8]{0:T(128)} %broadcast_multiply_fusion.factor_ref, bf16[96,1024]{1,0:T(8,128)(2,1)} %copy-done.5, bf16[2,256,3072]{2,1,0:T(8,128)(2,1)} %get-tuple-element.50.key_ref, bf16[2,3072,256]{2,1,0:T(8,128)(2,1)} %get-tuple-element.51.value_ref), custom_call_target="tpu_custom_call" | custom-call | tf_op jit(solution)/shard_map/attend/pallas_call | solution.py:276
  209.6 3.3 %collective-permute-start.12 = (bf16[96,1408]{1,0:T(8,128)(2,1)}, bf16[96,1408]{1,0:T(8,128)(2,1)S(1)}, u32[]{:S(2)}, u32[]{:S(2)}) collective-permute-start(bf16[96,1408]{1,0:T(8,128)(2,1)} %attend.5), channel_id=1, source_target_pairs={{0,96},{32,0},{64,32},{96,64},{1,97},{33,1},{65,33},{97,65},{2,98}... | collective-permute-start | bytes 811016 | tf_op jit(solution)/shard_map/ppermute | solution.py:285
  213.0 0.7 copy-done.4
  213.7 7.7 %attend.4 = bf16[96,1408]{1,0:T(8,128)(2,1)} custom-call(f32[8]{0:T(128)} %broadcast_multiply_fusion.factor_ref, bf16[96,1024]{1,0:T(8,128)(2,1)} %copy-done.4, bf16[2,256,3072]{2,1,0:T(8,128)(2,1)} %get-tuple-element.50.key_ref, bf16[2,3072,256]{2,1,0:T(8,128)(2,1)} %get-tuple-element.51.value_ref), custom_call_target="tpu_custom_call" | custom-call | tf_op jit(solution)/shard_map/attend/pallas_call | solution.py:276
  221.3 0.7 collective-permute-start.10
  222.0 7.7 %attend.7.d_ref = bf16[96,1408]{1,0:T(8,128)(2,1)} custom-call(f32[8]{0:T(128)} %broadcast_multiply_fusion.factor_ref, bf16[96,1024]{1,0:T(8,128)(2,1)} %get-tuple-element.49.query_ref, bf16[2,256,3072]{2,1,0:T(8,128)(2,1)} %get-tuple-element.50.key_ref, bf16[2,3072,256]{2,1,0:T(8,128)(2,1)} %get-tuple-element.51.value_ref), custom_call_target="tpu_custom_call" | custom-call | tf_op jit(solution)/shard_map/attend/pallas_call | solution.py:276
  229.7 0.6 collective-permute-done.10.a_ref
  230.3 0.1 copy-done.1
  230.4 0.1 copy-done.2
  230.5 0.5 copy-done.3
  231.0 3.7 %merge.1 = bf16[96,1024]{1,0:T(8,128)(2,1)} custom-call(bf16[96,1408]{1,0:T(8,128)(2,1)} %copy-done.3, bf16[96,1408]{1,0:T(8,128)(2,1)} %copy-done.2, bf16[96,1408]{1,0:T(8,128)(2,1)} %copy-done.1, bf16[96,1408]{1,0:T(8,128)(2,1)} %attend.7.d_ref, f32[96,1024]{1,0:T(8,128)} %get-tuple-element.52.coarse_ref, bf16[1024,1024]{1,0:T(8,128)(2,1)} %w_out_ref.1), custom_call_target="tpu_custom_call" | custom-call | tf_op jit(solution)/shard_map/merge/pallas_call | solution.py:287
  (48 shorter events, 0.8 us)
Async XLA Ops:
  0.6 16.2 %copy-start.8 = (s32[1,36864]{1,0:T(1,128)S(1)}, s32[1,36864]{1,0:T(1,128)}, u32[]{:S(2)}) copy-start(s32[1,36864]{1,0:T(1,128)} %param.26) | copy-start | bytes 442372
  0.6 16.2 %copy-start.7 = (s32[1,36864]{1,0:T(1,128)S(1)}, s32[1,36864]{1,0:T(1,128)}, u32[]{:S(2)}) copy-start(s32[1,36864]{1,0:T(1,128)} %param.27) | copy-start | bytes 442372
  4.7 40.0 %copy-start.11 = (s32[1,97]{1,0:T(1,128)S(1)}, s32[1,97]{1,0:T(1,128)}, u32[]{:S(2)}) copy-start(s32[1,97]{1,0:T(1,128)} %param.29) | copy-start | bytes 1168
  4.7 42.0 %collective-permute-start = (bf16[256,256]{1,0:T(8,128)(2,1)S(1)}, bf16[256,256]{1,0:T(8,128)(2,1)S(1)}, u32[]{:S(2)}, u32[]{:S(2)}) collective-permute-start(bf16[256,256]{1,0:T(8,128)(2,1)S(1)} %gather_fusion), channel_id=1, source_target_pairs={{0,1},{1,2},{2,3},{3,4},{4,5},{5,6},{6,7},{7,8},{8,9},{9,10},{10,1... | collective-permute-start | bytes 393224 | tf_op jit(solution)/shard_map/ppermute | solution.py:236
  8.0 38.7 %collective-permute-start.1 = (bf16[256,256]{1,0:T(8,128)(2,1)S(1)}, bf16[256,256]{1,0:T(8,128)(2,1)S(1)}, u32[]{:S(2)}, u32[]{:S(2)}) collective-permute-start(bf16[256,256]{1,0:T(8,128)(2,1)S(1)} %gather_fusion.1), channel_id=1, source_target_pairs={{0,127},{1,0},{2,1},{3,2},{4,3},{5,4},{6,5},{7,6},{8,7},{9,8},{10,... | collective-permute-start | bytes 393224 | tf_op jit(solution)/shard_map/ppermute | solution.py:237
  46.7 0.6 copy-start.9
  46.7 0.7 copy-start.10
  135.0 5.6 %collective-permute-start.2 = (bf16[1,104,256]{2,1,0:T(8,128)(2,1)}, bf16[1,104,256]{2,1,0:T(8,128)(2,1)S(1)}, u32[]{:S(2)}, u32[]{:S(2)}) collective-permute-start(bf16[1,104,256]{2,1,0:T(8,128)(2,1)} %bitcast.29), channel_id=1, source_target_pairs={{0,2},{1,3},{2,4},{3,5},{4,6},{5,7},{6,0},{7,1},{8,10},{9,11},{10,... | collective-permute-start | bytes 159752 | tf_op jit(solution)/shard_map/ppermute | solution.py:144
  135.7 4.9 %collective-permute-start.3 = (bf16[1,104,256]{2,1,0:T(8,128)(2,1)}, bf16[1,104,256]{2,1,0:T(8,128)(2,1)S(1)}, u32[]{:S(2)}, u32[]{:S(2)}) collective-permute-start(bf16[1,104,256]{2,1,0:T(8,128)(2,1)} %bitcast.30), channel_id=1, source_target_pairs={{0,6},{1,7},{2,0},{3,1},{4,2},{5,3},{6,4},{7,5},{8,14},{9,15},{10,... | collective-permute-start | bytes 159752 | tf_op jit(solution)/shard_map/ppermute | solution.py:144
  138.2 5.8 %collective-permute-start.4 = (bf16[1,104,256]{2,1,0:T(8,128)(2,1)}, bf16[1,104,256]{2,1,0:T(8,128)(2,1)S(1)}, u32[]{:S(2)}, u32[]{:S(2)}) collective-permute-start(bf16[1,104,256]{2,1,0:T(8,128)(2,1)} %bitcast.31), channel_id=1, source_target_pairs={{0,4},{1,5},{2,6},{3,7},{4,0},{5,1},{6,2},{7,3},{8,12},{9,13},{10,... | collective-permute-start | bytes 159752 | tf_op jit(solution)/shard_map/ppermute | solution.py:144
  144.9 7.1 %collective-permute-start.5 = (bf16[4,104,256]{2,1,0:T(8,128)(2,1)S(1)}, bf16[4,104,256]{2,1,0:T(8,128)(2,1)S(1)}, u32[]{:S(2)}, u32[]{:S(2)}) collective-permute-start(bf16[4,104,256]{2,1,0:T(8,128)(2,1)S(1)} %pad_maximum_fusion), channel_id=1, source_target_pairs={{0,8},{1,9},{2,10},{3,11},{4,12},{5,13},{6,14},{7,15},{8,16},{9,17... | collective-permute-start | bytes 638984 | tf_op jit(solution)/shard_map/ppermute | solution.py:147
  145.0 8.9 %collective-permute-start.6 = (bf16[4,104,256]{2,1,0:T(8,128)(2,1)S(1)}, bf16[4,104,256]{2,1,0:T(8,128)(2,1)S(1)}, u32[]{:S(2)}, u32[]{:S(2)}) collective-permute-start(bf16[4,104,256]{2,1,0:T(8,128)(2,1)S(1)} %pad_maximum_fusion), channel_id=1, source_target_pairs={{0,24},{1,25},{2,26},{3,27},{4,28},{5,29},{6,30},{7,31},{8,0},{9,1... | collective-permute-start | bytes 638984 | tf_op jit(solution)/shard_map/ppermute | solution.py:147
  148.2 7.3 %collective-permute-start.7 = (bf16[4,104,256]{2,1,0:T(8,128)(2,1)S(1)}, bf16[4,104,256]{2,1,0:T(8,128)(2,1)S(1)}, u32[]{:S(2)}, u32[]{:S(2)}) collective-permute-start(bf16[4,104,256]{2,1,0:T(8,128)(2,1)S(1)} %pad_maximum_fusion), channel_id=1, source_target_pairs={{0,16},{1,17},{2,18},{3,19},{4,20},{5,21},{6,22},{7,23},{8,24},{9,... | collective-permute-start | bytes 638984 | tf_op jit(solution)/shard_map/ppermute | solution.py:147
  155.6 2.5 %collective-permute-start.8 = (bf16[16,104,256]{2,1,0:T(8,128)(2,1)S(1)}, bf16[16,104,256]{2,1,0:T(8,128)(2,1)S(1)}, u32[]{:S(2)}, u32[]{:S(2)}) collective-permute-start(bf16[16,104,256]{2,1,0:T(8,128)(2,1)S(1)} %get-tuple-element.53), channel_id=1, source_target_pairs={{0,1},{1,0},{2,3},{3,2},{4,5},{5,4},{6,7},{7,6},{8,9},{9,8},{10,11... | collective-permute-start | bytes 2555912 | tf_op jit(solution)/shard_map/ppermute | solution.py:151
  158.1 1.2 copy-start
  159.3 8.5 %copy-start.12 = (f32[8]{0:T(128)S(1)}, f32[8]{0:T(128)}, u32[]{:S(2)}) copy-start(f32[8]{0:T(128)} %param.41) | copy-start | bytes 100
  163.8 29.1 %collective-permute-start.13 = (bf16[96,1024]{1,0:T(8,128)(2,1)}, bf16[96,1024]{1,0:T(8,128)(2,1)S(1)}, u32[]{:S(2)}, u32[]{:S(2)}) collective-permute-start(bf16[96,1024]{1,0:T(8,128)(2,1)} %get-tuple-element.49.query_ref), channel_id=1, source_target_pairs={{0,96},{32,0},{64,32},{96,64},{1,97},{33,1},{65,33},{97,65},{2,98}... | collective-permute-start | bytes 589832 | tf_op jit(solution)/shard_map/ppermute | solution.py:258
  163.8 37.4 %collective-permute-start.11 = (bf16[96,1024]{1,0:T(8,128)(2,1)}, bf16[96,1024]{1,0:T(8,128)(2,1)S(1)}, u32[]{:S(2)}, u32[]{:S(2)}) collective-permute-start(bf16[96,1024]{1,0:T(8,128)(2,1)} %get-tuple-element.49.query_ref), channel_id=1, source_target_pairs={{0,32},{32,64},{64,96},{96,0},{1,33},{33,65},{65,97},{97,1},{2,34}... | collective-permute-start | bytes 589832 | tf_op jit(solution)/shard_map/ppermute | solution.py:258
  165.8 47.2 %collective-permute-start.9 = (bf16[96,1024]{1,0:T(8,128)(2,1)}, bf16[96,1024]{1,0:T(8,128)(2,1)S(1)}, u32[]{:S(2)}, u32[]{:S(2)}) collective-permute-start(bf16[96,1024]{1,0:T(8,128)(2,1)} %get-tuple-element.49.query_ref), channel_id=1, source_target_pairs={{0,64},{32,96},{64,0},{96,32},{1,65},{33,97},{65,1},{97,33},{2,66}... | collective-permute-start | bytes 589832 | tf_op jit(solution)/shard_map/ppermute | solution.py:258
  192.8 0.7 copy-start.6
  201.2 28.5 %collective-permute-start.14 = (bf16[96,1408]{1,0:T(8,128)(2,1)}, bf16[96,1408]{1,0:T(8,128)(2,1)S(1)}, u32[]{:S(2)}, u32[]{:S(2)}) collective-permute-start(bf16[96,1408]{1,0:T(8,128)(2,1)} %attend.6), channel_id=1, source_target_pairs={{0,32},{32,64},{64,96},{96,0},{1,33},{33,65},{65,97},{97,1},{2,34}... | collective-permute-start | bytes 811016 | tf_op jit(solution)/shard_map/ppermute | solution.py:285
  201.3 0.7 copy-start.5
  209.6 20.1 %collective-permute-start.12 = (bf16[96,1408]{1,0:T(8,128)(2,1)}, bf16[96,1408]{1,0:T(8,128)(2,1)S(1)}, u32[]{:S(2)}, u32[]{:S(2)}) collective-permute-start(bf16[96,1408]{1,0:T(8,128)(2,1)} %attend.5), channel_id=1, source_target_pairs={{0,96},{32,0},{64,32},{96,64},{1,97},{33,1},{65,33},{97,65},{2,98}... | collective-permute-start | bytes 811016 | tf_op jit(solution)/shard_map/ppermute | solution.py:285
  213.0 0.7 copy-start.4
  221.3 9.0 %collective-permute-start.10 = (bf16[96,1408]{1,0:T(8,128)(2,1)}, bf16[96,1408]{1,0:T(8,128)(2,1)S(1)}, u32[]{:S(2)}, u32[]{:S(2)}) collective-permute-start(bf16[96,1408]{1,0:T(8,128)(2,1)} %attend.4), channel_id=1, source_target_pairs={{0,64},{32,96},{64,0},{96,32},{1,65},{33,97},{65,1},{97,33},{2,66}... | collective-permute-start | bytes 811016 | tf_op jit(solution)/shard_map/ppermute | solution.py:285
  229.7 0.7 copy-start.1
  229.7 0.8 copy-start.2
  230.3 0.7 copy-start.3

commit v2 on v1

v2 whole, which is shorter than its diff:
```python
import functools
import math
import jax, jax.numpy as jnp
from jax import lax
from jax.experimental import pallas as pl
from jax.experimental.pallas import tpu as pltpu
from jax.sharding import PartitionSpec as P

TILE = 256
WINDOW = 128
TOGETHER = 4
TARGET_SHIFT = 13
NO_TARGET = 6144
SLOT_ROWS = 104
bf16, f32, i32 = jnp.bfloat16, jnp.float32, jnp.int32


def sort_kernel(source_ref, target_ref, rows_ref, targets_ref, key):
    given = source_ref.shape[0]
    fill = jnp.full((8, 128), NO_TARGET << TARGET_SHIFT, i32)
    held = [(target_ref[v] << TARGET_SHIFT) | source_ref[v] if v < given else fill for v in range(64)]
    for phase in range(1, 6):
        for bit in range(phase - 1, -1, -1):
            for v in range(64):
                if not v >> bit & 1:
                    w = v | 1 << bit
                    small, large = jnp.minimum(held[v], held[w]), jnp.maximum(held[v], held[w])
                    held[v], held[w] = (large, small) if v >> phase & 1 else (small, large)
    for v in range(64):
        key[v >> 3, v & 7] = held[v]
    row = lax.broadcasted_iota(i32, (8, 128), 0)
    lane = lax.broadcasted_iota(i32, (8, 128), 1)

    def bit_of(bit):
        if bit == 16:
            return jnp.zeros((8, 128), i32)
        return (row >> (bit - 6) & 1) if bit < 9 else (lane >> (bit - 9) & 1)

    for phase in range(6, 17):
        flip = bit_of(phase) if phase == 6 else bit_of(phase) ^ bit_of(phase - 1)

        def across(g, carry):
            held = key[pl.ds(2 * g, 2)].reshape(16, 8, 128) ^ (-flip)[None]
            for bit in range(phase - 1, 5, -1):
                axis, by, size = (1, 1 << (bit - 6), 8) if bit < 9 else (2, 1 << (bit - 9), 128)
                upper = (bit_of(bit) == 1)[None]
                if 2 * by == size:
                    other = pltpu.roll(held, by, axis)
                else:
                    other = jnp.where(upper, pltpu.roll(held, by, axis), pltpu.roll(held, size - by, axis))
                held = jnp.where(upper, jnp.maximum(held, other), jnp.minimum(held, other))
            key[pl.ds(2 * g, 2)] = held.reshape(2, 8, 8, 128)
            return carry

        lax.fori_loop(0, 4, across, 0, unroll=4)

        def merge(held):
            for bit in (2, 1, 0):
                pairs = held.reshape(4 >> bit, 2, 1 << bit, 8, 128)
                held = jnp.stack(
                    [jnp.minimum(pairs[:, 0], pairs[:, 1]), jnp.maximum(pairs[:, 0], pairs[:, 1])], axis=1
                ).reshape(8, 8, 128)
            return held

        def high(g, carry):
            key[:, g] = merge(key[:, g])
            return carry

        def low(g, carry):
            key[g] = merge(key[g])
            return carry

        lax.fori_loop(0, 8, high, 0, unroll=8)
        lax.fori_loop(0, 8, low, 0, unroll=8)

    flat = key.reshape(512, 128)
    half = rows_ref.shape[1] // 2
    for part in range(4):
        piece = jnp.concatenate([flat[pl.ds(s, 64, stride=8), :] for s in (2 * part, 2 * part + 1)], axis=0)
        piece = jnp.transpose(piece)[:half]
        at = (part % 2, pl.ds(part // 2, half, stride=2), slice(None))
        rows_ref[at] = (piece & ((1 << TARGET_SHIFT) - 1)) * 2
        targets_ref[at] = piece >> TARGET_SHIFT


def sorted_edges(source, target):
    edges = source.shape[0]
    shape = jax.ShapeDtypeStruct((2, edges // TILE, 128), i32)
    return pl.pallas_call(
        sort_kernel,
        out_shape=(shape, shape),
        scratch_shapes=[pltpu.VMEM((8, 8, 8, 128), i32)],
        compiler_params=pltpu.CompilerParams(vmem_limit_bytes=24 << 20),
        name="sort_edges",
    )(source.reshape(-1, 8, 128), target.reshape(-1, 8, 128))


def fine_kernel(rows_ref, meta_ref, local_ref, slot_ref, tag_ref, own_ref, before_ref, after_ref, w_src_ref, w_dst_ref,
                bias_ref, w_msg_ref, w_upd_ref, out_ref, part_ref, table, dst, total, count, got_a, got_b):
    blocks = own_ref.shape[0] // TILE
    tiles_most = local_ref.shape[1]

    def put_table(place, rows):
        proj = jnp.dot(rows, w_src_ref[...], preferred_element_type=f32).astype(bf16).astype(f32) + bias_ref[...]
        table[pl.ds(2 * place, TILE, stride=2), :] = proj[:, :128]
        table[pl.ds(2 * place + 1, TILE, stride=2), :] = proj[:, 128:]

    def project(b, carry):
        at = pl.multiple_of(b * TILE, TILE)
        own = own_ref[pl.ds(at, TILE), :]
        put_table(at, own)
        dst[pl.ds(at, TILE), :] = jnp.dot(own, w_dst_ref[...], preferred_element_type=f32).astype(bf16)
        total[pl.ds(at, TILE), :] = jnp.zeros((TILE, 256), f32)
        count[pl.ds(at, TILE), :] = jnp.zeros((TILE, 128), f32)
        return carry

    lax.fori_loop(0, blocks, project, 0, unroll=4)
    put_table(blocks * TILE, before_ref[...])
    put_table(blocks * TILE + TILE, after_ref[...])

    place = lax.broadcasted_iota(i32, (WINDOW, TILE), 0).astype(f32).astype(bf16)
    one, zero = jnp.ones((WINDOW, TILE), bf16), jnp.zeros((WINDOW, TILE), bf16)
    ones = jnp.ones((TILE, 128), bf16)

    def fetch(base, first, last, got):
        for i in range(first, last):
            place = i % TILE // 128 * (tiles_most * 128) + i // TILE * 128 + i % 128
            got[2 * i:2 * i + 2, :] = table[pl.ds(rows_ref[base + place], 2), :]

    def tile_steps(tile, n, got, start):
        state = {}

        def first():
            state["at"] = at = pl.multiple_of(start, 16)
            local = jnp.concatenate([local_ref[k, pl.ds(tile, 1), :] for k in range(2)], axis=1)
            local = jnp.minimum(local - at, WINDOW).astype(f32).astype(bf16)
            state["hot"] = jnp.where(place == local, one, zero)
            state["own"] = lax.dot_general(
                state["hot"], dst[pl.ds(at, WINDOW), :], (((0,), (0,)), ((), ())), preferred_element_type=f32
            )

        def second():
            sent = [got[pl.ds(2 * TILE * n + k, TILE, stride=2), :] for k in range(2)]
            half = 0.5 * (state["own"] + jnp.concatenate(sent, axis=1))
            state["hidden"] = (half + half * jnp.tanh(half)).astype(bf16)

        def third():
            at = pl.ds(state["at"], WINDOW)
            total[at, :] += jnp.dot(state["hot"], state["hidden"], preferred_element_type=f32)
            count[at, :] += jnp.dot(state["hot"], ones, preferred_element_type=f32)

        return first, second, third

    def advance(tile, got, ahead, got_ahead):
        base = jnp.minimum(ahead, tiles_most - TOGETHER) * 128
        tiles = [tile_steps(tile + n, n, got, meta_ref[tile + n]) for n in range(TOGETHER)]
        steps = [run for steps in zip(*tiles) for run in steps]
        rows = TOGETHER * TILE
        for i, run in enumerate(steps):
            fetch(base, rows * i // len(steps), rows * (i + 1) // len(steps), got_ahead)
            run()

    def step(j, carry):
        tile = 2 * TOGETHER * j
        advance(tile, got_a, tile + TOGETHER, got_b)
        advance(tile + TOGETHER, got_b, tile + 2 * TOGETHER, got_a)
        return carry

    fetch(0, 0, TOGETHER * TILE, got_a)
    lax.fori_loop(0, meta_ref[2 * tiles_most], step, 0)

    def rest(tile, carry):
        def window(w, carry):
            fetch(tile * 128, 0, TILE, got_a)
            for run in tile_steps(tile, 0, got_a, jnp.minimum(meta_ref[tile] + w * WINDOW, blocks * TILE - WINDOW)):
                run()
            return carry

        return lax.fori_loop(1, meta_ref[tiles_most + tile], window, carry)

    lax.fori_loop(0, tiles_most, rest, 0)

    slots = lax.broadcasted_iota(i32, (SLOT_ROWS, TILE), 0)

    def finish(b, parts):
        at = pl.ds(pl.multiple_of(b * TILE, TILE), TILE)
        scale = 1.0 / jnp.maximum(count[at, :], 1.0)
        mean = total[at, :] * jnp.concatenate([scale, scale], axis=1)
        high = mean.astype(bf16)
        low = (mean - high.astype(f32)).astype(bf16)
        w_msg = w_msg_ref[...]
        agg = jnp.dot(high, w_msg, preferred_element_type=f32) + jnp.dot(low, w_msg, preferred_element_type=f32)
        update = jnp.dot(agg.astype(bf16), w_upd_ref[...], preferred_element_type=f32)
        new = (own_ref[at, :].astype(f32) + update).astype(bf16)
        out_ref[at, :] = new
        hot = (slots == slot_ref[b]).astype(f32).astype(bf16)
        return parts + jnp.dot(hot, new, preferred_element_type=f32)

    parts = lax.fori_loop(0, blocks, finish, tag_ref[...].astype(f32), unroll=4)
    part_ref[...] = parts.astype(bf16)


def fine_pass(own, before, after, source, target, cell_slot, tags, w_src, w_dst, bias, w_msg, w_upd):
    cells = own.shape[0]
    blocks = cells // TILE
    tiles = source.shape[0] // TILE
    rows, targets = sorted_edges(source, target)
    start = jnp.minimum(targets[0, :, 0] & -16, cells - WINDOW)
    last = jnp.max(jnp.where(targets < cells, targets, -1), axis=(0, 2))
    windows = jnp.maximum(last + WINDOW - start, 0) // WINDOW
    pairs = (jnp.sum((last >= 0).astype(i32)) + (2 * TOGETHER - 1)) // (2 * TOGETHER)
    meta = jnp.concatenate([start, windows, pairs[None]])
    smem = pl.BlockSpec(memory_space=pltpu.SMEM)
    vmem = pl.BlockSpec(memory_space=pltpu.VMEM)
    return pl.pallas_call(
        fine_kernel,
        out_shape=(jax.ShapeDtypeStruct(own.shape, bf16), jax.ShapeDtypeStruct((SLOT_ROWS, 256), bf16)),
        in_specs=[smem, smem] + [vmem] * 11,
        out_specs=(vmem, vmem),
        scratch_shapes=[
            pltpu.VMEM((2 * (cells + 2 * TILE), 128), f32),
            pltpu.VMEM((cells, 256), bf16),
            pltpu.VMEM((cells, 256), f32),
            pltpu.VMEM((cells, 128), f32),
            pltpu.VMEM((2 * TOGETHER * TILE, 128), f32),
            pltpu.VMEM((2 * TOGETHER * TILE, 128), f32),
        ],
        compiler_params=pltpu.CompilerParams(vmem_limit_bytes=58 << 20),
        name="fine_cells",
    )(rows.reshape(-1), meta, targets, cell_slot.reshape(blocks, 1, TILE), tags, own, before, after, w_src, w_dst,
      bias.reshape(1, -1), w_msg, w_upd)


def moved(value, axis, pairs):
    return lax.ppermute(value, axis, pairs)


def ring_gather(value, move):
    return jnp.concatenate([value] + [move(value, by) for by in (1, 3, 2)], axis=0)


def gather_group(part):
    devices = lax.axis_size("cur")

    def along_z(value, by):
        return lax.ppermute(value, "cur", [(i, i // 8 * 8 + (i + 2 * by) % 8) for i in range(devices)])

    def along_x(value, by):
        return lax.ppermute(value, "cur", [(i, (i + 8 * by) % devices) for i in range(devices)])

    rows = ring_gather(part[None], along_z)
    rows = ring_gather(rows, along_x)
    return jnp.concatenate([rows, lax.ppermute(rows, "cur", [(i, i ^ 1) for i in range(devices)])], axis=0)


def normed_parents(first, label_ref, rows_ref, w_pool_ref, gain_ref, parents):
    shape = (parents, rows_ref.shape[0])
    ids = lax.broadcasted_iota(i32, shape, 0).astype(f32).astype(bf16)
    label = jnp.clip(label_ref[...] - first, -1, 256).astype(f32).astype(bf16)
    hot = jnp.where(ids == label, jnp.ones(shape, bf16), jnp.zeros(shape, bf16))
    mean = (jnp.dot(hot, rows_ref[...], preferred_element_type=f32) * (1.0 / 64.0)).astype(bf16)
    coarse = jnp.dot(mean, w_pool_ref[...], preferred_element_type=f32)
    inverse = lax.rsqrt(jnp.mean(coarse * coarse, axis=1, keepdims=True) + 1e-06)
    return coarse, (coarse * inverse * gain_ref[...]).astype(bf16)


def query_kernel(first_ref, label_ref, rows_ref, w_pool_ref, gain_ref, w_query_ref, coarse_ref, query_ref):
    coarse, normed = normed_parents(first_ref[0], label_ref, rows_ref, w_pool_ref, gain_ref, query_ref.shape[0])
    coarse_ref[...] = coarse
    query_ref[...] = jnp.dot(normed, w_query_ref[...], preferred_element_type=f32).astype(bf16)


def key_kernel(first_ref, label_ref, rows_ref, w_pool_ref, gain_ref, w_key_ref, w_value_ref, key_ref, value_ref):
    most = 256
    for part in range(value_ref.shape[0] // most):
        at = slice(part * most, (part + 1) * most)
        first = first_ref[0] + pl.program_id(0) * value_ref.shape[0] + part * most
        coarse, normed = normed_parents(first, label_ref, rows_ref, w_pool_ref, gain_ref, most)
        keys = jnp.dot(normed, w_key_ref[...], preferred_element_type=f32)
        value_ref[at, :] = jnp.dot(normed, w_value_ref[...], preferred_element_type=f32).astype(bf16)
        key_ref[:, at] = jnp.transpose(keys).astype(bf16)


def attend_kernel(factor_ref, query_ref, key_a_ref, value_a_ref, key_b_ref, value_b_ref, out_ref):
    rows = query_ref.shape[0]
    chunk = value_a_ref.shape[0] // 2
    chunks = [(k, v, slice(c, c + chunk)) for k, v in ((key_a_ref, value_a_ref), (key_b_ref, value_b_ref)) for c in (0, chunk)]
    ones = jnp.ones((chunk, 128), bf16)
    stats, scores = [], []
    for g in range(2):
        scaled = jnp.concatenate(
            [query_ref[:, h * 128:(h + 1) * 128].astype(f32) * factor_ref[h] for h in range(4 * g, 4 * g + 4)], axis=0
        )
        high = scaled.astype(bf16)
        low = (scaled - high.astype(f32)).astype(bf16)
        query = jnp.concatenate([high, low], axis=1)
        own = slice(g * 128, (g + 1) * 128)
        scores.append(
            [jnp.dot(query, jnp.concatenate([k[own, c]] * 2, axis=0), preferred_element_type=f32) for k, v, c in chunks]
        )
    for g in range(2):
        own = slice(g * 128, (g + 1) * 128)
        tops = [jnp.max(score, axis=1, keepdims=True) for score in scores[g]]
        top = functools.reduce(jnp.maximum, tops)
        both = 0.0
        for score, (k, v, c) in zip(scores[g], chunks):
            weight = jnp.exp2(score - top).astype(bf16)
            both += jnp.dot(weight, jnp.concatenate([v[c, own], ones], axis=1), preferred_element_type=f32)
        norm = both[:, 128:]
        attn = (both[:, :128] / norm).astype(bf16)
        level = top + jnp.log2(norm)
        for r in range(4):
            h = 4 * g + r
            out_ref[:, h * 128:(h + 1) * 128] = attn[r * rows:(r + 1) * rows]
            stats.append(level[r * rows:(r + 1) * rows])
    lanes = lax.broadcasted_iota(i32, (rows, 128), 1)
    level = jnp.zeros((rows, 128), f32)
    for h in range(8):
        level = jnp.where(lanes == h, stats[h], level)
    high = level.astype(bf16)
    rest = level - high.astype(f32)
    middle = rest.astype(bf16)
    low = (rest - middle.astype(f32)).astype(bf16)
    out_ref[:, 1024:1152] = high
    out_ref[:, 1152:1280] = middle
    out_ref[:, 1280:1408] = low


def merge_kernel(a_ref, b_ref, c_ref, d_ref, coarse_ref, w_out_ref, out_ref):
    refs = (a_ref, b_ref, c_ref, d_ref)
    levels = [r[:, 1024:1152].astype(f32) + (r[:, 1152:1280].astype(f32) + r[:, 1280:1408].astype(f32)) for r in refs]
    top = jnp.maximum(jnp.maximum(levels[0], levels[1]), jnp.maximum(levels[2], levels[3]))
    shares = [jnp.exp2(level - top) for level in levels]
    whole = shares[0] + shares[1] + shares[2] + shares[3]
    shares = [share / whole for share in shares]
    pieces = []
    for h in range(8):
        at = slice(h * 128, (h + 1) * 128)
        pieces.append(sum(r[:, at].astype(f32) * s[:, h:h + 1] for r, s in zip(refs, shares)))
    attn = jnp.concatenate(pieces, axis=1).astype(bf16)
    out_ref[...] = (coarse_ref[...] + jnp.dot(attn, w_out_ref[...], preferred_element_type=f32)).astype(bf16)


def body(fine_state, send_index, edge_src, edge_dst, cell_slot, slot_parent, w_src, w_dst, msg_bias, w_msg, w_upd,
         w_pool, norm_gain, w_query, w_key, w_value, w_out, head_scale):
    groups, devices = lax.axis_size("grp"), lax.axis_size("cur")
    smem = pl.BlockSpec(memory_space=pltpu.SMEM)
    vmem = pl.BlockSpec(memory_space=pltpu.VMEM)
    every = groups * devices
    both = ("grp", "cur")
    before = lax.ppermute(fine_state[send_index[0, 0]], both, [(i, (i + 1) % every) for i in range(every)])
    after = lax.ppermute(fine_state[send_index[0, 1]], both, [(i, (i - 1) % every) for i in range(every)])
    slots = slot_parent.shape[1]
    par_dev = slots - 1
    parents = jnp.full((256,), -64, i32).at[:slots].set(slot_parent[0])
    tags = jnp.zeros((SLOT_ROWS, 256), i32).at[slots].set(parents >> 6).at[slots + 1].set(parents & 63).astype(bf16)
    fine_out, part = fine_pass(fine_state, before, after, edge_src[0], edge_dst[0], cell_slot, tags,
                               w_src, w_dst, msg_bias, w_msg, w_upd)
    blocks = gather_group(part)
    labels = (blocks[:, slots, :SLOT_ROWS].astype(i32) * 64 + blocks[:, slots + 1, :SLOT_ROWS].astype(i32)).reshape(1, -1)
    rows = blocks.reshape(-1, 256)
    gain = norm_gain.reshape(1, -1)
    width = w_query.shape[1]
    params = pltpu.CompilerParams(vmem_limit_bytes=56 << 20)
    coarse, query = pl.pallas_call(
        query_kernel,
        out_shape=(jax.ShapeDtypeStruct((par_dev, width), f32), jax.ShapeDtypeStruct((par_dev, width), bf16)),
        in_specs=[smem] + [vmem] * 5,
        out_specs=(vmem, vmem),
        compiler_params=params,
        name="own_query",
    )((lax.axis_index("cur") * par_dev)[None], labels, rows, w_pool, gain, w_query)
    asked = {by: lax.ppermute(query, "grp", [(i, (i + by) % groups) for i in range(groups)]) for by in (2, 1, 3)}
    asked[0] = query
    known = par_dev * devices // 2
    step = 512
    whole = lambda *shape: pl.BlockSpec(shape, lambda i: (0,) * len(shape))
    keys, values = pl.pallas_call(
        key_kernel,
        out_shape=(jax.ShapeDtypeStruct((256, known), bf16), jax.ShapeDtypeStruct((known, 256), bf16)),
        grid=(known // step,),
        in_specs=[smem, whole(*labels.shape), whole(*rows.shape), whole(*w_pool.shape), whole(*gain.shape),
                  whole(*w_key.shape), whole(*w_value.shape)],
        out_specs=(pl.BlockSpec((256, step), lambda i: (0, i)), pl.BlockSpec((step, 256), lambda i: (i, 0))),
        compiler_params=params,
        name="group_keys",
    )(((lax.axis_index("cur") & 1) * known)[None], labels, rows, w_pool, gain, w_key, w_value)
    swap = [(i, i ^ 1) for i in range(devices)]
    twin_keys, twin_values = lax.ppermute(keys, "cur", swap), lax.ppermute(values, "cur", swap)
    factor = head_scale * (math.log2(math.e) / math.sqrt(128.0))
    found = []
    for by in (2, 1, 3, 0):
        piece = pl.pallas_call(
            attend_kernel,
            out_shape=jax.ShapeDtypeStruct((par_dev, width + 384), bf16),
            in_specs=[smem] + [vmem] * 5,
            out_specs=vmem,
            compiler_params=params,
            name="attend",
        )(factor, asked[by], keys, values, twin_keys, twin_values)
        if by:
            piece = lax.ppermute(piece, "grp", [(i, (i - by) % groups) for i in range(groups)])
        found.append(piece)
    coarse_out = pl.pallas_call(
        merge_kernel,
        out_shape=jax.ShapeDtypeStruct((par_dev, width), bf16),
        in_specs=[vmem] * 6,
        out_specs=vmem,
        compiler_params=params,
        name="merge",
    )(*found, coarse, w_out)
    return fine_out, coarse_out


def solution(mesh):
    line = P(("grp", "cur"), None)
    in_specs = (line, P(("grp", "cur"), None, None), line, line, P(("grp", "cur")), line) + (P(),) * 12
    return jax.shard_map(body, mesh=mesh, in_specs=in_specs, out_specs=(line, line), check_vma=False)
```

time: 238 us -> 178 us (0.75); the launches traced: 235 us -> 178 us
  Pallas kernels: 151 us -> 114 us
  other arithmetic: 31.1 us -> 4.35 us
  waiting for transfers between devices: 15.1 us -> 23 us
  starting transfers between devices: 23.7 us -> 21 us
    pallas_call x1, Pallas kernels: 87.6 us -> 58.4 us  [fine_pass(): pl.pallas_call(fine_kernel, out_shape=(jax.ShapeDtypeStruct(own.shape, bf...]
    sort x1 -> x0, other arithmetic: 25.2 us -> none  [sort_edges(): keys = jnp.sort(jnp.concatenate([key, filler.reshape(-1)]))]
    pallas_call x4, Pallas kernels: 30.6 us -> 21.7 us  [body(): pl.pallas_call(attend_kernel, out_shape=jax.ShapeDtypeStruct((par_dev, wi...]
    ppermute x3, waiting for transfers between devices: 0.01 us -> 5.76 us  [body(): lax.ppermute(query, 'grp', [(i, (i + by) % groups) for i in range(groups)])]
    unnamed x33 -> x40, local copies, waits for them, and re-layouts: 4.64 us -> 6.47 us
    pallas_call x1 -> x2, Pallas kernels: 24.5 us -> 25.3 us  [the longest x1 14.5 us: body(): pl.pallas_call(key_kernel, out_shape=(jax.ShapeDtypeStruct((256, known),...]
  transfers between devices with their start and end apart: 15 -> 17, of which waited for: 7 -> 6; matrix products, arithmetic and copies ran while one was open for 14% -> 4% of each run, Pallas kernels for 23% -> 21%
where the time goes in v2:
time: 178 us
  Pallas kernels  114 us (64%)
  waiting for transfers between devices  23 us (13%)
  starting transfers between devices  21 us (12%)
  local copies, waits for them, and re-layouts  14 us (8%)
  other arithmetic  4.35 us (2%)
    pallas_call x1, Pallas kernels, fine_pass(): pl.pallas_call(fine_kernel, out_shape=(jax.ShapeDtypeStruct(own.shape, bf...  58.4 us
    pallas_call x4, Pallas kernels, body(): pl.pallas_call(attend_kernel, out_shape=jax.ShapeDtypeStruct((par_dev, wi...  21.7 us
    pallas_call x1, Pallas kernels, body(): pl.pallas_call(key_kernel, out_shape=(jax.ShapeDtypeStruct((256, known),...  14.5 us
    pallas_call x1, Pallas kernels, sorted_edges(): pl.pallas_call(sort_kernel, out_shape=(shape, shape), scratch_shapes=[plt...  10.8 us
    ppermute x1, starting transfers between devices, body(): lax.ppermute(fine_state[send_index[0, 1]], both, [(i, (i - 1) % every) fo...  8.27 us
    ppermute x3, waiting for transfers between devices, along_x(): lax.ppermute(value, 'cur', [(i, (i + 8 * by) % devices) for i in range(de...  7.52 us
    unnamed x40, local copies, waits for them, and re-layouts  6.47 us
    ppermute x3, waiting for transfers between devices, body(): lax.ppermute(query, 'grp', [(i, (i + by) % groups) for i in range(groups)])  5.76 us
  transfers between devices with their start and end apart: 17, of which 6 were waited for; matrix products, arithmetic and copies ran while one was open for 4% of the time, Pallas kernels for 21%

profile of v2, /device:TPU:0, one launch (start us, length us, event | category | flops | bytes accessed | tf_op | source)
XLA Modules:
  0.0 177.6 jit_solution(10150553101610620515)
XLA Ops:
  0.7 0.8 compare_select_fusion.1
  1.4 3.3 %gather_fusion = bf16[256,256]{1,0:T(8,128)(2,1)S(1)} fusion(bf16[6144,256]{1,0:T(8,128)(2,1)} %own_ref.1, s32[1024]{0:T(1024)S(1)} %get-tuple-element.75), kind=kCustom, calls=%fused_computation | custom fusion | bytes 263168 | tf_op jit(solution)/shard_map/gather | solution.py:351
  4.7 0.1 collective-permute-start
  4.8 3.3 %gather_fusion.1 = bf16[256,256]{1,0:T(8,128)(2,1)S(1)} fusion(bf16[6144,256]{1,0:T(8,128)(2,1)} %own_ref.1, s32[1024]{0:T(1024)S(1)} %get-tuple-element.74), kind=kCustom, calls=%fused_computation.1 | custom fusion | bytes 263168 | tf_op jit(solution)/shard_map/gather | solution.py:352
  8.0 8.3 %collective-permute-start.1 = (bf16[256,256]{1,0:T(8,128)(2,1)S(1)}, bf16[256,256]{1,0:T(8,128)(2,1)S(1)}, u32[]{:S(2)}, u32[]{:S(2)}) collective-permute-start(bf16[256,256]{1,0:T(8,128)(2,1)S(1)} %gather_fusion.1), channel_id=1, source_target_pairs={{0,127},{1,0},{2,1},{3,2},{4,3},{5,4},{6,5},{7,6},{8,7},{9,8},{10,... | collective-permute-start | bytes 393224 | tf_op jit(solution)/shard_map/ppermute | solution.py:352
  16.3 10.8 %sort_edges.1 = (s32[2,144,128]{2,1,0:T(8,128)S(1)}, s32[2,144,128]{2,1,0:T(8,128)S(1)}) custom-call(s32[36,8,128]{2,1,0:T(8,128)S(1)} %bitcast.23, s32[36,8,128]{2,1,0:T(8,128)S(1)} %bitcast.24), custom_call_target="tpu_custom_call" | custom-call | tf_op jit(solution)/shard_map/sort_edges/pallas_call | solution.py:89
  27.2 0.7 copy-done.1
  27.8 0.1 minimum_reduce_fusion
  27.9 0.1 fusion
  28.1 0.6 and_select_fusion
  29.4 0.6 convert_element_type.29.tag_ref
  30.1 0.7 pad_add_fusion.meta_ref
  30.8 0.6 copy-done.13
  31.4 58.4 %fine_cells.1 = (bf16[6144,256]{1,0:T(8,128)(2,1)}, bf16[104,256]{1,0:T(8,128)(2,1)}) custom-call(s32[36864]{0:T(1024)} %bitcast.22, s32[289]{0:T(512)} %pad_add_fusion.meta_ref, s32[2,144,128]{2,1,0:T(8,128)} %copy-done, s32[24,1,256]{2,1,0:T(1,128)} %bitcast.31, bf16[104,256]{1,0:T(8,128)(2,1)} %convert_element_type.29.tag_ref, bf16[6144,256]{1,0:T(8,128)(2,1)} %own_ref.1, ...), custom_call_target="tpu_custom_call" | custom-call | tf_op jit(solution)/shard_map/fine_cells/pallas_call | solution.py:215
  89.9 3.2 %collective-permute-start.3 = (bf16[1,104,256]{2,1,0:T(8,128)(2,1)}, bf16[1,104,256]{2,1,0:T(8,128)(2,1)S(1)}, u32[]{:S(2)}, u32[]{:S(2)}) collective-permute-start(bf16[1,104,256]{2,1,0:T(8,128)(2,1)} %bitcast.28), channel_id=1, source_target_pairs={{0,6},{1,7},{2,0},{3,1},{4,2},{5,3},{6,4},{7,5},{8,14},{9,15},{10,... | collective-permute-start | bytes 159752 | tf_op jit(solution)/shard_map/ppermute | solution.py:246
  93.1 0.9 constant_dynamic-update-slice_fusion.6
  94.0 1.4 collective-permute-done.2
  95.4 3.5 %collective-permute-done.4 = bf16[1,104,256]{2,1,0:T(8,128)(2,1)S(1)} collective-permute-done((bf16[1,104,256]{2,1,0:T(8,128)(2,1)}, bf16[1,104,256]{2,1,0:T(8,128)(2,1)S(1)}, u32[]{:S(2)}, u32[]{:S(2)}) %collective-permute-start.4) | collective-permute-done | bytes 53280 | tf_op jit(solution)/shard_map/ppermute | solution.py:246
  98.9 0.8 pad_maximum_fusion
  99.8 0.1 collective-permute-start.5
  99.9 3.2 %collective-permute-start.6 = (bf16[4,104,256]{2,1,0:T(8,128)(2,1)S(1)}, bf16[4,104,256]{2,1,0:T(8,128)(2,1)S(1)}, u32[]{:S(2)}, u32[]{:S(2)}) collective-permute-start(bf16[4,104,256]{2,1,0:T(8,128)(2,1)S(1)} %pad_maximum_fusion), channel_id=1, source_target_pairs={{0,24},{1,25},{2,26},{3,27},{4,28},{5,29},{6,30},{7,31},{8,0},{9,1... | collective-permute-start | bytes 638984 | tf_op jit(solution)/shard_map/ppermute | solution.py:249
  103.1 7.5 %collective-permute-done.5 = bf16[4,104,256]{2,1,0:T(8,128)(2,1)S(1)} collective-permute-done((bf16[4,104,256]{2,1,0:T(8,128)(2,1)S(1)}, bf16[4,104,256]{2,1,0:T(8,128)(2,1)S(1)}, u32[]{:S(2)}, u32[]{:S(2)}) %collective-permute-start.5) | collective-permute-done | bytes 213024 | tf_op jit(solution)/shard_map/ppermute | solution.py:249
  110.8 0.1 collective-permute-start.8
  110.9 2.4 %collective-permute-done.8 = bf16[16,104,256]{2,1,0:T(8,128)(2,1)S(1)} collective-permute-done((bf16[16,104,256]{2,1,0:T(8,128)(2,1)S(1)}, bf16[16,104,256]{2,1,0:T(8,128)(2,1)S(1)}, u32[]{:S(2)}, u32[]{:S(2)}) %collective-permute-start.8) | collective-permute-done | bytes 852000 | tf_op jit(solution)/shard_map/ppermute | solution.py:253
  113.3 0.1 fusion.2
  113.4 0.9 add.60.label_ref
  114.3 0.2 copy-done.6
  114.5 14.5 %group_keys.1 = (bf16[256,1536]{1,0:T(8,128)(2,1)}, bf16[1536,256]{1,0:T(8,128)(2,1)}) custom-call(s32[1]{0:T(128)} %bitcast.17.first_ref, s32[1,3328]{1,0:T(1,128)} %add.60.label_ref, bf16[3328,256]{1,0:T(8,128)(2,1)} %bitcast.25, bf16[256,1024]{1,0:T(8,128)(2,1)} %w_pool_ref.3, f32[1,1024]{1,0:T(1,128)} %bitcast.32, bf16[1024,256]{1,0:T(8,128)(2,1)} %w_key_ref.1, ...), custom_call_target="tpu_custom_call" | custom-call | tf_op jit(solution)/shard_map/group_keys/pallas_call | solution.py:378
  129.0 0.1 collective-permute-start.10
  129.1 0.4 collective-permute-start.11
  129.5 4.4 %own_query.1 = (f32[96,1024]{1,0:T(8,128)}, bf16[96,1024]{1,0:T(8,128)(2,1)}) custom-call(s32[1]{0:T(128)} %bitcast.13.first_ref, s32[1,3328]{1,0:T(1,128)} %add.60.label_ref, bf16[3328,256]{1,0:T(8,128)(2,1)} %bitcast.26, bf16[256,1024]{1,0:T(8,128)(2,1)} %w_pool_ref.3, f32[1,1024]{1,0:T(1,128)} %bitcast.33, bf16[1024,1024]{1,0:T(8,128)(2,1)} %w_query_ref.1), custom_call_target="tpu_custom_call" | custom-call | tf_op jit(solution)/shard_map/own_query/pallas_call | solution.py:365
  133.9 0.4 collective-permute-start.13
  134.3 2.8 %collective-permute-start.15 = (bf16[96,1024]{1,0:T(8,128)(2,1)}, bf16[96,1024]{1,0:T(8,128)(2,1)S(1)}, u32[]{:S(2)}, u32[]{:S(2)}) collective-permute-start(bf16[96,1024]{1,0:T(8,128)(2,1)} %get-tuple-element.50.query_ref), channel_id=1, source_target_pairs={{0,96},{32,0},{64,32},{96,64},{1,97},{33,1},{65,33},{97,65},{2,98}... | collective-permute-start | bytes 589832 | tf_op jit(solution)/shard_map/ppermute | solution.py:373
  137.1 0.5 broadcast_multiply_fusion.factor_ref
  137.7 5.8 %collective-permute-done.9.query_ref = bf16[96,1024]{1,0:T(8,128)(2,1)S(1)} collective-permute-done((bf16[96,1024]{1,0:T(8,128)(2,1)}, bf16[96,1024]{1,0:T(8,128)(2,1)S(1)}, u32[]{:S(2)}, u32[]{:S(2)}) %collective-permute-start.9) | collective-permute-done | bytes 196640 | tf_op jit(solution)/shard_map/ppermute | solution.py:373
  143.4 0.7 copy-done.12
  144.1 0.3 copy-done.4
  144.4 0.9 copy-done.5
  145.3 5.4 %attend.4 = bf16[96,1408]{1,0:T(8,128)(2,1)} custom-call(f32[8]{0:T(128)} %broadcast_multiply_fusion.factor_ref, bf16[96,1024]{1,0:T(8,128)(2,1)} %copy-done.12, bf16[256,1536]{1,0:T(8,128)(2,1)} %get-tuple-element.51.key_a_ref, bf16[1536,256]{1,0:T(8,128)(2,1)} %get-tuple-element.52.value_a_ref, bf16[256,1536]{1,0:T(8,128)(2,1)} %copy-done.4, ...), custom_call_target="tpu_custom_call" | custom-call | tf_op jit(solution)/shard_map/attend/pallas_call | solution.py:393
  150.7 0.7 copy-done.11
  151.4 5.4 %attend.5 = bf16[96,1408]{1,0:T(8,128)(2,1)} custom-call(f32[8]{0:T(128)} %broadcast_multiply_fusion.factor_ref, bf16[96,1024]{1,0:T(8,128)(2,1)} %copy-done.11, bf16[256,1536]{1,0:T(8,128)(2,1)} %get-tuple-element.51.key_a_ref, bf16[1536,256]{1,0:T(8,128)(2,1)} %get-tuple-element.52.value_a_ref, bf16[256,1536]{1,0:T(8,128)(2,1)} %copy-done.4, ...), custom_call_target="tpu_custom_call" | custom-call | tf_op jit(solution)/shard_map/attend/pallas_call | solution.py:393
  156.8 2.3 %collective-permute-start.14 = (bf16[96,1408]{1,0:T(8,128)(2,1)}, bf16[96,1408]{1,0:T(8,128)(2,1)S(1)}, u32[]{:S(2)}, u32[]{:S(2)}) collective-permute-start(bf16[96,1408]{1,0:T(8,128)(2,1)} %attend.5), channel_id=1, source_target_pairs={{0,96},{32,0},{64,32},{96,64},{1,97},{33,1},{65,33},{97,65},{2,98}... | collective-permute-start | bytes 811016 | tf_op jit(solution)/shard_map/ppermute | solution.py:402
  159.2 0.7 copy-done.10
  159.8 5.4 %attend.6 = bf16[96,1408]{1,0:T(8,128)(2,1)} custom-call(f32[8]{0:T(128)} %broadcast_multiply_fusion.factor_ref, bf16[96,1024]{1,0:T(8,128)(2,1)} %copy-done.10, bf16[256,1536]{1,0:T(8,128)(2,1)} %get-tuple-element.51.key_a_ref, bf16[1536,256]{1,0:T(8,128)(2,1)} %get-tuple-element.52.value_a_ref, bf16[256,1536]{1,0:T(8,128)(2,1)} %copy-done.4, ...), custom_call_target="tpu_custom_call" | custom-call | tf_op jit(solution)/shard_map/attend/pallas_call | solution.py:393
  165.3 5.4 %attend.7.d_ref = bf16[96,1408]{1,0:T(8,128)(2,1)} custom-call(f32[8]{0:T(128)} %broadcast_multiply_fusion.factor_ref, bf16[96,1024]{1,0:T(8,128)(2,1)} %get-tuple-element.50.query_ref, bf16[256,1536]{1,0:T(8,128)(2,1)} %get-tuple-element.51.key_a_ref, bf16[1536,256]{1,0:T(8,128)(2,1)} %get-tuple-element.52.value_a_ref, bf16[256,1536]{1,0:T(8,128)(2,1)} %copy-done.4, ...), custom_call_target="tpu_custom_call" | custom-call | tf_op jit(solution)/shard_map/attend/pallas_call | solution.py:393
  170.7 2.4 %collective-permute-done.16.c_ref = bf16[96,1408]{1,0:T(8,128)(2,1)S(1)} collective-permute-done((bf16[96,1408]{1,0:T(8,128)(2,1)}, bf16[96,1408]{1,0:T(8,128)(2,1)S(1)}, u32[]{:S(2)}, u32[]{:S(2)}) %collective-permute-start.16) | collective-permute-done | bytes 270368 | tf_op jit(solution)/shard_map/ppermute | solution.py:402
  173.2 0.7 copy-done.9
  173.9 3.7 %merge.1 = bf16[96,1024]{1,0:T(8,128)(2,1)} custom-call(bf16[96,1408]{1,0:T(8,128)(2,1)} %copy-done.7, bf16[96,1408]{1,0:T(8,128)(2,1)} %copy-done.8, bf16[96,1408]{1,0:T(8,128)(2,1)} %copy-done.9, bf16[96,1408]{1,0:T(8,128)(2,1)} %attend.7.d_ref, f32[96,1024]{1,0:T(8,128)} %get-tuple-element.53.coarse_ref, bf16[1024,1024]{1,0:T(8,128)(2,1)} %w_out_ref.1), custom_call_target="tpu_custom_call" | custom-call | tf_op jit(solution)/shard_map/merge/pallas_call | solution.py:404
  (53 shorter events, 0.4 us)
Async XLA Ops:
  0.6 15.7 %copy-start.2 = (s32[1,36864]{1,0:T(1,128)S(1)}, s32[1,36864]{1,0:T(1,128)}, u32[]{:S(2)}) copy-start(s32[1,36864]{1,0:T(1,128)} %param.26) | copy-start | bytes 442372
  0.6 15.7 %copy-start.3 = (s32[1,36864]{1,0:T(1,128)S(1)}, s32[1,36864]{1,0:T(1,128)}, u32[]{:S(2)}) copy-start(s32[1,36864]{1,0:T(1,128)} %param.27) | copy-start | bytes 442372
  0.7 28.1 %copy-start.15 = (s32[1,97]{1,0:T(1,128)S(1)}, s32[1,97]{1,0:T(1,128)}, u32[]{:S(2)}) copy-start(s32[1,97]{1,0:T(1,128)} %param.29) | copy-start | bytes 1168
  4.7 26.0 %collective-permute-start = (bf16[256,256]{1,0:T(8,128)(2,1)S(1)}, bf16[256,256]{1,0:T(8,128)(2,1)S(1)}, u32[]{:S(2)}, u32[]{:S(2)}) collective-permute-start(bf16[256,256]{1,0:T(8,128)(2,1)S(1)} %gather_fusion), channel_id=1, source_target_pairs={{0,1},{1,2},{2,3},{3,4},{4,5},{5,6},{6,7},{7,8},{8,9},{9,10},{10,1... | collective-permute-start | bytes 393224 | tf_op jit(solution)/shard_map/ppermute | solution.py:351
  8.0 22.7 %collective-permute-start.1 = (bf16[256,256]{1,0:T(8,128)(2,1)S(1)}, bf16[256,256]{1,0:T(8,128)(2,1)S(1)}, u32[]{:S(2)}, u32[]{:S(2)}) collective-permute-start(bf16[256,256]{1,0:T(8,128)(2,1)S(1)} %gather_fusion.1), channel_id=1, source_target_pairs={{0,127},{1,0},{2,1},{3,2},{4,3},{5,4},{6,5},{7,6},{8,7},{9,8},{10,... | collective-permute-start | bytes 393224 | tf_op jit(solution)/shard_map/ppermute | solution.py:352
  27.2 0.7 copy-start.1
  27.8 2.9 %copy-start = (s32[2,144,128]{2,1,0:T(8,128)}, s32[2,144,128]{2,1,0:T(8,128)S(1)}, u32[]{:S(2)}) copy-start(s32[2,144,128]{2,1,0:T(8,128)S(1)} %get-tuple-element.47.local_ref) | copy-start | bytes 442372
  30.7 0.7 copy-start.13
  30.7 0.7 copy-start.14
  89.9 5.6 %collective-permute-start.2 = (bf16[1,104,256]{2,1,0:T(8,128)(2,1)}, bf16[1,104,256]{2,1,0:T(8,128)(2,1)S(1)}, u32[]{:S(2)}, u32[]{:S(2)}) collective-permute-start(bf16[1,104,256]{2,1,0:T(8,128)(2,1)} %bitcast.27), channel_id=1, source_target_pairs={{0,2},{1,3},{2,4},{3,5},{4,6},{5,7},{6,0},{7,1},{8,10},{9,11},{10,... | collective-permute-start | bytes 159752 | tf_op jit(solution)/shard_map/ppermute | solution.py:246
  89.9 5.6 %collective-permute-start.3 = (bf16[1,104,256]{2,1,0:T(8,128)(2,1)}, bf16[1,104,256]{2,1,0:T(8,128)(2,1)S(1)}, u32[]{:S(2)}, u32[]{:S(2)}) collective-permute-start(bf16[1,104,256]{2,1,0:T(8,128)(2,1)} %bitcast.28), channel_id=1, source_target_pairs={{0,6},{1,7},{2,0},{3,1},{4,2},{5,3},{6,4},{7,5},{8,14},{9,15},{10,... | collective-permute-start | bytes 159752 | tf_op jit(solution)/shard_map/ppermute | solution.py:246
  93.1 5.8 %collective-permute-start.4 = (bf16[1,104,256]{2,1,0:T(8,128)(2,1)}, bf16[1,104,256]{2,1,0:T(8,128)(2,1)S(1)}, u32[]{:S(2)}, u32[]{:S(2)}) collective-permute-start(bf16[1,104,256]{2,1,0:T(8,128)(2,1)} %bitcast.29), channel_id=1, source_target_pairs={{0,4},{1,5},{2,6},{3,7},{4,0},{5,1},{6,2},{7,3},{8,12},{9,13},{10,... | collective-permute-start | bytes 159752 | tf_op jit(solution)/shard_map/ppermute | solution.py:246
  99.8 10.9 %collective-permute-start.5 = (bf16[4,104,256]{2,1,0:T(8,128)(2,1)S(1)}, bf16[4,104,256]{2,1,0:T(8,128)(2,1)S(1)}, u32[]{:S(2)}, u32[]{:S(2)}) collective-permute-start(bf16[4,104,256]{2,1,0:T(8,128)(2,1)S(1)} %pad_maximum_fusion), channel_id=1, source_target_pairs={{0,8},{1,9},{2,10},{3,11},{4,12},{5,13},{6,14},{7,15},{8,16},{9,17... | collective-permute-start | bytes 638984 | tf_op jit(solution)/shard_map/ppermute | solution.py:249
  99.9 10.8 %collective-permute-start.6 = (bf16[4,104,256]{2,1,0:T(8,128)(2,1)S(1)}, bf16[4,104,256]{2,1,0:T(8,128)(2,1)S(1)}, u32[]{:S(2)}, u32[]{:S(2)}) collective-permute-start(bf16[4,104,256]{2,1,0:T(8,128)(2,1)S(1)} %pad_maximum_fusion), channel_id=1, source_target_pairs={{0,24},{1,25},{2,26},{3,27},{4,28},{5,29},{6,30},{7,31},{8,0},{9,1... | collective-permute-start | bytes 638984 | tf_op jit(solution)/shard_map/ppermute | solution.py:249
  103.1 7.6 %collective-permute-start.7 = (bf16[4,104,256]{2,1,0:T(8,128)(2,1)S(1)}, bf16[4,104,256]{2,1,0:T(8,128)(2,1)S(1)}, u32[]{:S(2)}, u32[]{:S(2)}) collective-permute-start(bf16[4,104,256]{2,1,0:T(8,128)(2,1)S(1)} %pad_maximum_fusion), channel_id=1, source_target_pairs={{0,16},{1,17},{2,18},{3,19},{4,20},{5,21},{6,22},{7,23},{8,24},{9,... | collective-permute-start | bytes 638984 | tf_op jit(solution)/shard_map/ppermute | solution.py:249
  110.8 2.5 %collective-permute-start.8 = (bf16[16,104,256]{2,1,0:T(8,128)(2,1)S(1)}, bf16[16,104,256]{2,1,0:T(8,128)(2,1)S(1)}, u32[]{:S(2)}, u32[]{:S(2)}) collective-permute-start(bf16[16,104,256]{2,1,0:T(8,128)(2,1)S(1)} %get-tuple-element.54), channel_id=1, source_target_pairs={{0,1},{1,0},{2,3},{3,2},{4,5},{5,4},{6,7},{7,6},{8,9},{9,8},{10,11... | collective-permute-start | bytes 2555912 | tf_op jit(solution)/shard_map/ppermute | solution.py:253
  113.3 1.2 copy-start.6
  129.0 14.4 %collective-permute-start.10 = (bf16[256,1536]{1,0:T(8,128)(2,1)}, bf16[256,1536]{1,0:T(8,128)(2,1)S(1)}, u32[]{:S(2)}, u32[]{:S(2)}) collective-permute-start(bf16[256,1536]{1,0:T(8,128)(2,1)} %get-tuple-element.51.key_a_ref), channel_id=1, source_target_pairs={{0,1},{1,0},{2,3},{3,2},{4,5},{5,4},{6,7},{7,6},{8,9},{9,8},{10,11... | collective-permute-start | bytes 2359304 | tf_op jit(solution)/shard_map/ppermute | solution.py:389
  129.1 14.3 %collective-permute-start.11 = (bf16[1536,256]{1,0:T(8,128)(2,1)}, bf16[1536,256]{1,0:T(8,128)(2,1)S(1)}, u32[]{:S(2)}, u32[]{:S(2)}) collective-permute-start(bf16[1536,256]{1,0:T(8,128)(2,1)} %get-tuple-element.52.value_a_ref), channel_id=1, source_target_pairs={{0,1},{1,0},{2,3},{3,2},{4,5},{5,4},{6,7},{7,6},{8,9},{9,8},{10,11... | collective-permute-start | bytes 2359304 | tf_op jit(solution)/shard_map/ppermute | solution.py:389
  129.5 7.7 %copy-start.16 = (f32[8]{0:T(128)S(1)}, f32[8]{0:T(128)}, u32[]{:S(2)}) copy-start(f32[8]{0:T(128)} %param.41) | copy-start | bytes 100
  133.9 9.5 %collective-permute-start.9 = (bf16[96,1024]{1,0:T(8,128)(2,1)}, bf16[96,1024]{1,0:T(8,128)(2,1)S(1)}, u32[]{:S(2)}, u32[]{:S(2)}) collective-permute-start(bf16[96,1024]{1,0:T(8,128)(2,1)} %get-tuple-element.50.query_ref), channel_id=1, source_target_pairs={{0,64},{32,96},{64,0},{96,32},{1,65},{33,97},{65,1},{97,33},{2,66}... | collective-permute-start | bytes 589832 | tf_op jit(solution)/shard_map/ppermute | solution.py:373
  133.9 16.8 %collective-permute-start.13 = (bf16[96,1024]{1,0:T(8,128)(2,1)}, bf16[96,1024]{1,0:T(8,128)(2,1)S(1)}, u32[]{:S(2)}, u32[]{:S(2)}) collective-permute-start(bf16[96,1024]{1,0:T(8,128)(2,1)} %get-tuple-element.50.query_ref), channel_id=1, source_target_pairs={{0,32},{32,64},{64,96},{96,0},{1,33},{33,65},{65,97},{97,1},{2,34}... | collective-permute-start | bytes 589832 | tf_op jit(solution)/shard_map/ppermute | solution.py:373
  134.3 24.8 %collective-permute-start.15 = (bf16[96,1024]{1,0:T(8,128)(2,1)}, bf16[96,1024]{1,0:T(8,128)(2,1)S(1)}, u32[]{:S(2)}, u32[]{:S(2)}) collective-permute-start(bf16[96,1024]{1,0:T(8,128)(2,1)} %get-tuple-element.50.query_ref), channel_id=1, source_target_pairs={{0,96},{32,0},{64,32},{96,64},{1,97},{33,1},{65,33},{97,65},{2,98}... | collective-permute-start | bytes 589832 | tf_op jit(solution)/shard_map/ppermute | solution.py:373
  143.4 0.7 copy-start.12
  143.4 1.0 copy-start.4
  144.4 0.9 copy-start.5
  150.7 20.0 %collective-permute-start.12 = (bf16[96,1408]{1,0:T(8,128)(2,1)}, bf16[96,1408]{1,0:T(8,128)(2,1)S(1)}, u32[]{:S(2)}, u32[]{:S(2)}) collective-permute-start(bf16[96,1408]{1,0:T(8,128)(2,1)} %attend.4), channel_id=1, source_target_pairs={{0,64},{32,96},{64,0},{96,32},{1,65},{33,97},{65,1},{97,33},{2,66}... | collective-permute-start | bytes 811016 | tf_op jit(solution)/shard_map/ppermute | solution.py:402
  150.7 0.7 copy-start.11
  156.8 13.9 %collective-permute-start.14 = (bf16[96,1408]{1,0:T(8,128)(2,1)}, bf16[96,1408]{1,0:T(8,128)(2,1)S(1)}, u32[]{:S(2)}, u32[]{:S(2)}) collective-permute-start(bf16[96,1408]{1,0:T(8,128)(2,1)} %attend.5), channel_id=1, source_target_pairs={{0,96},{32,0},{64,32},{96,64},{1,97},{33,1},{65,33},{97,65},{2,98}... | collective-permute-start | bytes 811016 | tf_op jit(solution)/shard_map/ppermute | solution.py:402
  159.2 0.7 copy-start.10
  165.3 7.9 %collective-permute-start.16 = (bf16[96,1408]{1,0:T(8,128)(2,1)}, bf16[96,1408]{1,0:T(8,128)(2,1)S(1)}, u32[]{:S(2)}, u32[]{:S(2)}) collective-permute-start(bf16[96,1408]{1,0:T(8,128)(2,1)} %attend.6), channel_id=1, source_target_pairs={{0,32},{32,64},{64,96},{96,0},{1,33},{33,65},{65,97},{97,1},{2,34}... | collective-permute-start | bytes 811016 | tf_op jit(solution)/shard_map/ppermute | solution.py:402
  170.7 2.4 %copy-start.7 = (bf16[96,1408]{1,0:T(8,128)(2,1)}, bf16[96,1408]{1,0:T(8,128)(2,1)S(1)}, u32[]{:S(2)}) copy-start(bf16[96,1408]{1,0:T(8,128)(2,1)S(1)} %collective-permute-done.12.a_ref) | copy-start | bytes 811012
  170.7 2.4 %copy-start.8 = (bf16[96,1408]{1,0:T(8,128)(2,1)}, bf16[96,1408]{1,0:T(8,128)(2,1)S(1)}, u32[]{:S(2)}) copy-start(bf16[96,1408]{1,0:T(8,128)(2,1)S(1)} %collective-permute-done.14.b_ref) | copy-start | bytes 811012
  173.2 0.7 copy-start.9
